TPU v7x, 256 devices: a whole 4x4x8 slice. The times are simulated.
256 devices in a mesh: tm: 2 (over core), height: 32 (over z, x), tensor: 4 (over y).
Axes of the slice: x: 4, y: 4, z: 8, core: 2. Of those that a mesh axis runs over, the one named last changes fastest.
Arguments:
- queries: bfloat16 [2, 32, 1, 256, 3072], P('tm', 'height', None, None, 'tensor'), may hold values from -8 to 8
- key_rows: bfloat16 [2, 32, 1, 256, 3072], P('tm', 'height', None, None, 'tensor'), may hold values from -6 to 6
- value_rows: bfloat16 [2, 32, 1, 256, 3072], P('tm', 'height', None, None, 'tensor'), may hold values from -6 to 6
- grad_output: bfloat16 [2, 32, 1, 256, 3072], P('tm', 'height', None, 'tensor'), may hold values from -6 to 6
- out_weight: bfloat16 [3072, 3072], P('tensor'), may hold values from -0.109375 to 0.109375
- window_flags: int32 [2, 32, 1, 9], replicated, may hold values from 0 to 1, as said below
- valid_counts: int32 [2, 32, 1], replicated, may hold values from 32 to 256, as said below
Outputs:
- grad_queries: bfloat16 [2, 32, 1, 256, 3072], P('tm', 'height', None, None, 'tensor')
- grad_keys: bfloat16 [2, 32, 1, 256, 3072], P('tm', 'height', None, None, 'tensor')
- value_rows_gradient: bfloat16 [2, 32, 1, 256, 3072], P('tm', 'height', None, None, 'tensor')
Inputs may be any that keep to these rules, and one draw needn't show every extreme that they name: `window_flags`: slot s stands for the tile offset (s // 3 - 1 in time, s % 3 - 1 in height); slot 4, the tile itself, is always 1; a slot whose tile lies outside the grid is 0. `valid_counts`: tokens at a position within the tile at or beyond the count are padding; some tiles are full.
All inputs are finite; a program needn't handle non-finite values.
Results may differ from a plain program's by a relative error of at most 0.012.
Values may be sent and summed in bfloat16 or wider, within the bound.
A program may use at most 128 MiB of HBM per device.

v0:
```python
import jax
import jax.numpy as jnp
from jax import lax
from jax.sharding import PartitionSpec as P

HD = 128


WINDOW_OFFSETS = ((-1, -1), (-1, 0), (-1, 1), (0, -1), (0, 0), (0, 1), (1, -1), (1, 0), (1, 1))
MASKED_SCORE = -1e30


def extended(x, sides, width):
    for axis, dim in sides:
        size, length = (lax.axis_size(axis), x.shape[dim])
        up = [(i, (i + 1) % size) for i in range(size - 1)]
        down = [(j, i) for i, j in up]
        last = lax.slice_in_dim(x, length - width, length, axis=dim)
        leading = lax.slice_in_dim(x, 0, width, axis=dim)
        before = lax.ppermute(last, axis, up)
        after = lax.ppermute(leading, axis, down)
        x = jnp.concatenate([before, x, after], axis=dim)
    return x


def from_behind(x, axis, by):
    size = lax.axis_size(axis)
    pairs = [(i, i + by) for i in range(size) if 0 <= i + by < size]
    return lax.ppermute(x, axis, pairs)


def query_side(query_tile, pair_nine, grad_tile, allowed):
    tile_length, feature_width = query_tile.shape
    head_count = feature_width // HD
    softmax_scale = HD ** (-0.5)
    query_heads = query_tile.reshape(tile_length, head_count, HD)
    key_heads = pair_nine[:, 0].reshape(9 * tile_length, head_count, HD)
    value_heads = pair_nine[:, 1].reshape(9 * tile_length, head_count, HD)
    grad_heads = grad_tile.reshape(tile_length, head_count, HD)
    mask_bias = jnp.where(allowed, 0.0, MASKED_SCORE).astype(jnp.float32)
    scores = (
        jnp.einsum("qhd,khd->hqk", query_heads, key_heads, preferred_element_type=jnp.float32)
        * softmax_scale
        + mask_bias[None, None, :]
    )
    row_max = jnp.max(scores, axis=-1, keepdims=True)
    row_total = jnp.sum(jnp.exp(scores - row_max), axis=-1, keepdims=True)
    inverse_total = 1.0 / row_total
    softmax = jnp.exp(scores - row_max) * inverse_total
    grad_probs = jnp.einsum(
        "qhd,khd->hqk", grad_heads, value_heads, preferred_element_type=jnp.float32
    )
    row_delta = jnp.sum(softmax * grad_probs, axis=-1, keepdims=True)
    grad_scores = (softmax * (grad_probs - row_delta)).astype(jnp.bfloat16)
    query_gradient = (
        jnp.einsum("hqk,khd->qhd", grad_scores, key_heads, preferred_element_type=jnp.float32)
        * softmax_scale
    )
    query_gradient = query_gradient.astype(jnp.bfloat16).reshape(tile_length, feature_width)
    probs_low = softmax.astype(jnp.bfloat16)
    grad_key = (
        jnp.einsum("hqk,qhd->khd", grad_scores, query_heads, preferred_element_type=jnp.float32)
        * softmax_scale
    )
    value_gradient = jnp.einsum(
        "hqk,qhd->khd", probs_low, grad_heads, preferred_element_type=jnp.float32
    )
    return (
        query_gradient,
        jnp.stack(
            (
                grad_key.reshape(9, tile_length, feature_width),
                value_gradient.reshape(9, tile_length, feature_width),
            ),
            axis=1,
        ),
    )


def local(queries, key_rows, value_rows, grad_output, out_weight, window_flags, valid_counts):
    time_tiles, row_tiles, col_tiles, tile_length, feature_width = queries.shape
    tile_total = time_tiles * row_tiles * col_tiles
    grad_attn = jnp.einsum(
        "abcrd,fd->abcrf",
        lax.all_gather(grad_output, "tensor", axis=3, tiled=True),
        out_weight,
        preferred_element_type=jnp.float32,
    ).astype(jnp.bfloat16)
    time_start = lax.axis_index("tm") * time_tiles
    row_start = lax.axis_index("height") * row_tiles
    anchor = time_start * 0
    valid_ext = lax.dynamic_slice(
        jnp.pad(valid_counts, ((1, 1), (1, 1), (0, 0))),
        (time_start, row_start, anchor),
        (time_tiles + 2, row_tiles + 2, col_tiles),
    )
    flags_ext = lax.dynamic_slice(
        jnp.pad(window_flags, ((1, 1), (1, 1), (0, 0), (0, 0))),
        (time_start, row_start, anchor, anchor),
        (time_tiles + 2, row_tiles + 2, col_tiles, 9),
    )
    positions = lax.broadcasted_iota(jnp.int32, (tile_length,), 0)
    pairs = jnp.stack((key_rows, value_rows), axis=3)
    pairs_ext = extended(pairs, (("tm", 0), ("height", 1)), 1)
    pair_nine = jnp.stack(
        [
            pairs_ext[
                1 + time_off : 1 + time_off + time_tiles, 1 + row_off : 1 + row_off + row_tiles
            ]
            for time_off, row_off in WINDOW_OFFSETS
        ],
        axis=3,
    )
    count_nine = jnp.stack(
        [
            valid_ext[
                1 + time_off : 1 + time_off + time_tiles, 1 + row_off : 1 + row_off + row_tiles
            ]
            for time_off, row_off in WINDOW_OFFSETS
        ],
        axis=3,
    )
    own_flags = flags_ext[1:-1, 1:-1]
    allowed = (own_flags[..., None] > 0) & (positions < count_nine[..., None])
    flat_inputs = (
        queries.reshape(tile_total, tile_length, feature_width),
        pair_nine.reshape(tile_total, 9, 2, tile_length, feature_width),
        grad_attn.reshape(tile_total, tile_length, feature_width),
        allowed.reshape(tile_total, 9 * tile_length),
    )

    def with_grads(operands):
        return query_side(operands[0], operands[1], operands[2], operands[3])

    full_query_gradient, pieces = lax.map(with_grads, flat_inputs)
    pieces = pieces.reshape(time_tiles, row_tiles, col_tiles, 9, 2, tile_length, feature_width)
    spread = jnp.zeros(
        (time_tiles + 2, row_tiles + 2, col_tiles, 2, tile_length, feature_width), jnp.float32
    )
    for slot_index, (time_off, row_off) in enumerate(WINDOW_OFFSETS):
        spread = spread.at[
            1 + time_off : 1 + time_off + time_tiles, 1 + row_off : 1 + row_off + row_tiles
        ].add(pieces[:, :, :, slot_index])
    folded_rows = spread[:, 1:-1]
    for direction in (1, -1):
        outgoing = spread[:, -1] if direction == 1 else spread[:, 0]
        arrived = from_behind(outgoing.astype(jnp.bfloat16), "height", direction).astype(
            outgoing.dtype
        )
        folded_rows = (
            folded_rows.at[:, 0].add(arrived)
            if direction == 1
            else folded_rows.at[:, -1].add(arrived)
        )
    folded = folded_rows[1:-1]
    for direction in (1, -1):
        outgoing = folded_rows[-1] if direction == 1 else folded_rows[0]
        arrived = from_behind(outgoing.astype(jnp.bfloat16), "tm", direction).astype(outgoing.dtype)
        folded = folded.at[0].add(arrived) if direction == 1 else folded.at[-1].add(arrived)
    grad_queries = full_query_gradient.reshape(queries.shape)
    grad_keys = folded[:, :, :, 0].astype(jnp.bfloat16)
    value_rows_gradient = folded[:, :, :, 1].astype(jnp.bfloat16)
    return (grad_queries, grad_keys, value_rows_gradient)


def solution(mesh):
    placed = (
        P("tm", "height", None, None, "tensor"),
        P("tm", "height", None, None, "tensor"),
        P("tm", "height", None, None, "tensor"),
        P("tm", "height", None, "tensor", None),
        P("tensor", None),
        P(),
        P(),
    )
    return jax.shard_map(
        local,
        mesh=mesh,
        in_specs=placed,
        out_specs=(
            P("tm", "height", None, None, "tensor"),
            P("tm", "height", None, None, "tensor"),
            P("tm", "height", None, None, "tensor"),
        ),
        check_vma=False,
    )
```

profile of v0, /device:TPU:129, one launch (start us, length us, event | category | flops | bytes accessed | tf_op | source)
XLA Modules:
  0.0 355.1 jit_solution(2455431316908867509)
XLA Ops:
  15.3 2.8 pad_maximum_fusion
  18.1 3.1 collective-permute-start.2
  21.2 5.5 %collective-permute-start.3 = (bf16[3,1,1,2,256,768]{5,4,3,2,1,0:T(8,128)(2,1)}, bf16[3,1,1,2,256,768]{5,4,3,2,1,0:T(8,128)(2,1)}, u32[]{:S(2)}, u32[]{:S(2)}) collective-permute-start(bf16[3,1,1,2,256,768]{5,4,3,2,1,0:T(8,128)(2,1)} %pad_maximum_fusion), channel_id=1, source_target_pairs={{4,0},{8,4},{12,8},{16,12},{20,16},{24,20},{28,24},{32,28},{36,32}... | collective-permute-start | bytes 7077896 | tf_op jit(solution)/shard_map/ppermute | solution.py:21
  30.7 5.9 %stack.97 = s32[1,1,1,9]{3,2,1,0:T(1,128)S(1)} concatenate(s32[1,1,1,1]{3,2,1,0:T(1,128)} %bitcast.13, s32[1,1,1,1]{3,2,1,0:T(1,128)} %bitcast.14, s32[1,1,1,1]{3,2,1,0:T(1,128)} %bitcast.15, s32[1,1,1,1]{3,2,1,0:T(1,128)} %bitcast.16, s32[1,1,1,1]{3,2,1,0:T(1,128)} %bitcast.17, s32[1,1,1,1]{3,2,1,0:T(1,128)} %bitcast.18, s32[1,1,1,1]{3,2,1,0:T(1,128)} %bitcast.19, ...), dimensions={3} | concatenate | bytes 72 | tf_op jit(solution)/shard_map/stack | solution.py:114
  39.7 4.0 %all-gather.2.cloned.1.call-done = bf16[1,1,1,256,3072]{4,3,2,1,0:T(8,128)(2,1)} async-done(((bf16[1,1,1,64,3072]{4,3,2,1,0:T(8,128)(2,1)}), bf16[1,1,1,256,3072]{4,3,2,1,0:T(8,128)(2,1)}) %all-gather.2.cloned.1.call-update) | async-done | bytes 1572880 | tf_op jit(solution)/shard_map/all_gather | solution.py:85
  43.7 4.2 %fusion.35 = bf16[256,768]{1,0:T(8,128)(2,1)S(1)} fusion(bf16[768,3072]{1,0:T(8,128)(2,1)} %param.37, bf16[1,1,1,256,3072]{4,3,2,1,0:T(8,128)(2,1)} %all-gather.2.cloned.1.call-done), kind=kOutput, calls=%fused_computation.58 | convolution fusion | flops 1208156160 | bytes 6684672 | tf_op jit(solution)/shard_map/abcrd,fd->abcrf/dot_general | solution.py:83
  48.9 27.5 %collective-permute-done.2 = bf16[3,1,1,2,256,768]{5,4,3,2,1,0:T(8,128)(2,1)} collective-permute-done((bf16[3,1,1,2,256,768]{5,4,3,2,1,0:T(8,128)(2,1)}, bf16[3,1,1,2,256,768]{5,4,3,2,1,0:T(8,128)(2,1)}, u32[]{:S(2)}, u32[]{:S(2)}) %collective-permute-start.2) | collective-permute-done | bytes 2359328 | tf_op jit(solution)/shard_map/ppermute | solution.py:20
  85.9 5.9 %squeeze.22 = bf16[2304,6,128]{2,1,0:T(8,128)(2,1)} reshape(bf16[9,1,256,768]{3,2,1,0:T(8,128)(2,1)S(1)} %get-tuple-element.191) | data formatting | bytes 7077888 | tf_op jit(solution)/shard_map/while/body/eval_jaxpr/reshape;while/body/eval_jaxpr/squeeze | solution.py:37
  91.8 5.2 %copy.48 = bf16[2304,6,128]{0,2,1:T(8,128)(2,1)S(1)} copy(bf16[2304,6,128]{2,1,0:T(8,128)(2,1)} %squeeze.22) | data formatting | bytes 7077888 | tf_op jit(solution)/shard_map/while/body/eval_jaxpr/reshape;while/body/eval_jaxpr/squeeze | solution.py:37
  97.0 8.4 %fusion.59 = f32[6,2304,256]{2,1,0:T(8,128)} fusion(bf16[2304,6,128]{0,2,1:T(8,128)(2,1)S(1)} %copy.48, bf16[256,6,128]{0,2,1:T(8,128)(2,1)} %bitcast.232), kind=kOutput, calls=%fused_computation.104 | convolution fusion | flops 905969664 | bytes 18087936 | tf_op jit(solution)/shard_map/while/body/eval_jaxpr/qhd,khd->hqk/dot_general | solution.py:42
  105.4 11.3 %fusion.58 = (f32[6,256]{1,0:T(8,128)}, f32[6,256,2304]{1,2,0:T(8,128)}) fusion(f32[2304]{0:T(1024)S(1)} %and_select_fusion, bf16[2304,6,128]{0,2,1:T(8,128)(2,1)S(1)} %copy.48, bf16[256,6,128]{0,2,1:T(8,128)(2,1)} %bitcast.233), kind=kOutput, calls=%fused_computation.103 | convolution fusion | flops 920127744 | bytes 18103296 | tf_op jit(solution)/shard_map/while/body/eval_jaxpr/sub | solution.py:49
  117.4 8.4 %squeeze.23 = bf16[2304,6,128]{2,1,0:T(8,128)(2,1)} reshape(bf16[9,1,256,768]{3,2,1,0:T(8,128)(2,1)} %get-tuple-element.190) | data formatting | bytes 7077888 | tf_op jit(solution)/shard_map/while/body/eval_jaxpr/reshape;while/body/eval_jaxpr/squeeze | solution.py:38
  125.8 17.0 %fusion.9 = f32[2304,6,128]{0,2,1:T(8,128)} fusion(bf16[256,6,128]{0,2,1:T(8,128)(2,1)S(1)} %bitcast.242, f32[6,256]{1,0:T(8,128)S(1)} %broadcast_divide_fusion, f32[6,2304,256]{2,1,0:T(8,128)} %fusion.59, f32[2304]{0:T(1024)S(1)} %and_select_fusion), kind=kOutput, calls=%fused_computation.15 | convolution fusion | flops 930746112 | bytes 21642240 | tf_op jit(solution)/shard_map/while/body/eval_jaxpr/hqk,qhd->khd/dot_general | solution.py:65
  142.8 8.8 %copy.53 = f32[2304,6,128]{2,1,0:T(8,128)} copy(f32[2304,6,128]{0,2,1:T(8,128)} %fusion.9) | data formatting | bytes 14155776 | tf_op jit(solution)/shard_map/while/body/eval_jaxpr/hqk,qhd->khd/transpose | solution.py:65
  151.6 9.3 %reshape.840 = f32[9,1,256,768]{3,2,0,1:T(8,128)} reshape(f32[2304,6,128]{2,1,0:T(8,128)} %copy.53) | data formatting | bytes 14155776 | tf_op jit(solution)/shard_map/while/body/eval_jaxpr/stack;while/body/eval_jaxpr/reshape | solution.py:70
  160.9 12.8 %multiply_reduce_fusion = (f32[6,256]{1,0:T(8,128)S(1)}, f32[6,256,2304]{1,2,0:T(8,128)}) fusion(f32[6,256,2304]{1,2,0:T(8,128)} %get-tuple-element.208, f32[6,256]{1,0:T(8,128)S(1)} %broadcast_divide_fusion, bf16[256,6,128]{0,2,1:T(8,128)(2,1)S(1)} %bitcast.243, bf16[2304,6,128]{2,1,0:T(8,128)(2,1)} %squeeze.23), kind=kOutput, calls=%fused_computation.7 | convolution fusion | flops 916584960 | bytes 32256000 | tf_op jit(solution)/shard_map/while/body/eval_jaxpr/qhd,khd->hqk/dot_general | solution.py:50
  176.3 6.6 %multiply_convert_fusion = bf16[6,256,2304]{1,2,0:T(8,128)(2,1)S(1)} fusion(f32[6,256,2304]{1,2,0:T(8,128)} %get-tuple-element.210, f32[6,256,2304]{1,2,0:T(8,128)S(1)} %bitcast.229, f32[6,256]{1,0:T(8,128)S(1)} %get-tuple-element.209, f32[6,256]{1,0:T(8,128)S(1)} %broadcast_divide_fusion), kind=kLoop, calls=%fused_computation.6 | loop fusion | flops 14155776 | bytes 35401728 | tf_op jit(solution)/shard_map/while/body/eval_jaxpr/convert_element_type | solution.py:54
  185.9 14.0 %copy.51 = f32[2304,6,128]{2,1,0:T(8,128)} copy(f32[2304,6,128]{2,0,1:T(8,128)S(1)} %multiply_bitcast_fusion) | data formatting | bytes 14155776 | tf_op jit(solution)/shard_map/while/body/eval_jaxpr/mul | solution.py:62
  199.9 9.3 %reshape.839 = f32[9,1,256,768]{3,2,0,1:T(8,128)} reshape(f32[2304,6,128]{2,1,0:T(8,128)} %copy.51) | data formatting | bytes 14155776 | tf_op jit(solution)/shard_map/while/body/eval_jaxpr/stack;while/body/eval_jaxpr/reshape | solution.py:70
  209.2 11.3 %maximum_bitcast_fusion = f32[1,1,1,9,2,256,768]{6,5,3,4,2,1,0:T(8,128)} fusion(f32[9,1,256,768]{3,2,0,1:T(8,128)} %reshape.840, f32[9,1,256,768]{3,2,0,1:T(8,128)} %reshape.839), kind=kLoop, calls=%fused_computation.1 | loop fusion | flops 3538944 | bytes 28311552 | tf_op jit(solution)/shard_map/reshape | solution.py:136
  221.9 8.6 %scatter-add.30 = f32[3,3,1,2,256,768]{5,4,3,2,1,0:T(8,128)} pad(f32[1,1,1,2,256,768]{5,4,3,2,1,0:T(8,128)S(1)} %slice_bitcast_fusion.11, f32[]{:T(128)} %constant.392.clone.1), padding=0_2x0_2x0_0x0_0x0_0x0_0 | pad | bytes 15728644 | tf_op jit(solution)/shard_map/scatter-add | solution.py:143
  234.7 4.7 %fusion.14 = f32[3,3,1,2,256,768]{5,4,3,2,1,0:T(8,128)} fusion(f32[3,3,1,2,256,768]{5,4,3,2,1,0:T(8,128)} %fusion.16, s32[]{:T(128)} %bitcast.35, s32[]{:T(128)} %bitcast.36, f32[1,1,1,9,2,256,768]{6,5,3,4,2,1,0:T(8,128)S(1)} %copy-done.1, pred[]{:T(512)} %and_reduce_fusion), kind=kLoop, calls=%fused_computation.26 | loop fusion | flops 786432 | bytes 4720128 | tf_op jit(solution)/shard_map/scatter-add | solution.py:143
  242.1 2.8 fusion.28
  244.9 2.8 fusion.26
  250.4 2.8 fusion.22
  253.1 2.7 fusion.20
  255.9 8.9 %convert.24 = bf16[3,3,1,2,256,768]{5,4,3,2,1,0:T(8,128)(2,1)} convert(f32[3,3,1,2,256,768]{5,4,3,2,1,0:T(8,128)} %fusion.20) | non-fusion elementwise | flops 3538944 | bytes 21233664 | tf_op jit(solution)/shard_map/convert.9
  267.5 7.0 %collective-permute-start.5 = (bf16[3,1,2,256,768]{4,3,2,0,1:T(8,128)(2,1)S(1)}, bf16[3,1,2,256,768]{4,3,2,0,1:T(8,128)(2,1)S(1)}, u32[]{:S(2)}, u32[]{:S(2)}) collective-permute-start(bf16[3,1,2,256,768]{4,3,2,0,1:T(8,128)(2,1)S(1)} %get-tuple-element.189), channel_id=1, source_target_pairs={{4,0},{8,4},{12,8},{16,12},{20,16},{24,20},{28,24},{32,28},{36,32}... | collective-permute-start | bytes 7077896 | tf_op jit(solution)/shard_map/ppermute | solution.py:29
  276.9 46.9 %collective-permute-done.5 = bf16[3,1,2,256,768]{4,3,2,0,1:T(8,128)(2,1)S(1)} collective-permute-done((bf16[3,1,2,256,768]{4,3,2,0,1:T(8,128)(2,1)S(1)}, bf16[3,1,2,256,768]{4,3,2,0,1:T(8,128)(2,1)S(1)}, u32[]{:S(2)}, u32[]{:S(2)}) %collective-permute-start.5) | collective-permute-done | bytes 2359328 | tf_op jit(solution)/shard_map/ppermute | solution.py:29
  323.7 7.5 %collective-permute-done.4 = bf16[3,1,2,256,768]{4,3,2,0,1:T(8,128)(2,1)S(1)} collective-permute-done((bf16[3,1,2,256,768]{4,3,2,0,1:T(8,128)(2,1)S(1)}, bf16[3,1,2,256,768]{4,3,2,0,1:T(8,128)(2,1)S(1)}, u32[]{:S(2)}, u32[]{:S(2)}) %collective-permute-start.4) | collective-permute-done | bytes 2359328 | tf_op jit(solution)/shard_map/ppermute | solution.py:29
  331.2 5.5 %fusion.33 = (bf16[3,1,1,2,256,768]{5,4,3,0,2,1:T(8,128)(2,1)S(1)}, f32[3,1,1,2,256,768]{5,4,3,2,1,0:T(8,128)}) fusion(bf16[3,1,2,256,768]{4,3,2,0,1:T(8,128)(2,1)S(1)} %collective-permute-done.5, bf16[3,1,2,256,768]{4,3,2,0,1:T(8,128)(2,1)S(1)} %collective-permute-done.4, f32[3,3,1,2,256,768]{5,4,3,2,1,0:T(8,128)} %fusion.20), kind=kLoop, calls=%fused_computation.55 | loop fusion | flops 5898240 | bytes 16515072 | tf_op jit(solution)/shard_map/convert.7
  336.7 4.4 %collective-permute-start.7 = (bf16[1,1,2,256,768]{4,3,2,1,0:T(8,128)(2,1)S(1)}, bf16[1,1,2,256,768]{4,3,2,1,0:T(8,128)(2,1)S(1)}, u32[]{:S(2)}, u32[]{:S(2)}) collective-permute-start(bf16[1,1,2,256,768]{4,3,2,1,0:T(8,128)(2,1)S(1)} %slice_bitcast_fusion.12), channel_id=1, source_target_pairs={{128,0},{129,1},{130,2},{131,3},{132,4},{133,5},{134,6},{135,7},{1... | collective-permute-start | bytes 2359304 | tf_op jit(solution)/shard_map/ppermute | solution.py:29
  (87 shorter events, 54.7 us)
Async XLA Ops:
  7.2 31.8 %copy-start.9 = (s32[6]{0:T(128)S(1)}, s32[6]{0:T(128)}, u32[]{:S(2)}) copy-start(s32[6]{0:T(128)} %constant.398.clone.1) | copy-start | bytes 76
  7.2 29.5 %copy-start.8 = (bf16[1,1,1,256,768]{4,3,2,1,0:T(8,128)(2,1)S(1)}, bf16[1,1,1,256,768]{4,3,2,1,0:T(8,128)(2,1)}, u32[]{:S(2)}) copy-start(bf16[1,1,1,256,768]{4,3,2,1,0:T(8,128)(2,1)} %param.33) | copy-start | bytes 1179652
  7.2 36.5 %all-gather.2.cloned.1.call-start = ((), (), s32[]{:S(2)}) async-start(), calls=%async_computation | async-start | bytes 1966080 | tf_op jit(solution)/shard_map/all_gather | solution.py:85
  8.5 4.5 %collective-permute-start.1 = (bf16[1,1,1,2,256,768]{5,4,3,2,1,0:T(8,128)(2,1)S(1)}, bf16[1,1,1,2,256,768]{5,4,3,2,1,0:T(8,128)(2,1)S(1)}, u32[]{:S(2)}, u32[]{:S(2)}) collective-permute-start(bf16[1,1,1,2,256,768]{5,4,3,2,1,0:T(8,128)(2,1)S(1)} %pad_maximum_fusion.1), channel_id=1, source_target_pairs={{128,0},{129,1},{130,2},{131,3},{132,4},{133,5},{134,6},{135,7},{1... | collective-permute-start | bytes 2359304 | tf_op jit(solution)/shard_map/ppermute | solution.py:21
  11.1 4.2 %collective-permute-start = (bf16[1,1,1,2,256,768]{5,4,3,2,1,0:T(8,128)(2,1)S(1)}, bf16[1,1,1,2,256,768]{5,4,3,2,1,0:T(8,128)(2,1)S(1)}, u32[]{:S(2)}, u32[]{:S(2)}) collective-permute-start(bf16[1,1,1,2,256,768]{5,4,3,2,1,0:T(8,128)(2,1)S(1)} %pad_maximum_fusion.1), channel_id=1, source_target_pairs={{0,128},{1,129},{2,130},{3,131},{4,132},{5,133},{6,134},{7,135},{8... | collective-permute-start | bytes 2359304 | tf_op jit(solution)/shard_map/ppermute | solution.py:20
  18.1 58.2 %collective-permute-start.2 = (bf16[3,1,1,2,256,768]{5,4,3,2,1,0:T(8,128)(2,1)}, bf16[3,1,1,2,256,768]{5,4,3,2,1,0:T(8,128)(2,1)}, u32[]{:S(2)}, u32[]{:S(2)}) collective-permute-start(bf16[3,1,1,2,256,768]{5,4,3,2,1,0:T(8,128)(2,1)} %pad_maximum_fusion), channel_id=1, source_target_pairs={{0,4},{4,8},{8,12},{12,16},{16,20},{20,24},{24,28},{28,32},{32,36}... | collective-permute-start | bytes 7077896 | tf_op jit(solution)/shard_map/ppermute | solution.py:20
  21.2 56.4 %collective-permute-start.3 = (bf16[3,1,1,2,256,768]{5,4,3,2,1,0:T(8,128)(2,1)}, bf16[3,1,1,2,256,768]{5,4,3,2,1,0:T(8,128)(2,1)}, u32[]{:S(2)}, u32[]{:S(2)}) collective-permute-start(bf16[3,1,1,2,256,768]{5,4,3,2,1,0:T(8,128)(2,1)} %pad_maximum_fusion), channel_id=1, source_target_pairs={{4,0},{8,4},{12,8},{16,12},{20,16},{24,20},{28,24},{32,28},{36,32}... | collective-permute-start | bytes 7077896 | tf_op jit(solution)/shard_map/ppermute | solution.py:21
  39.7 40.3 %copy-start.5 = (bf16[1,1,1,256,768]{4,3,2,1,0:T(8,128)(2,1)S(1)}, bf16[1,1,1,256,768]{4,3,2,1,0:T(8,128)(2,1)}, u32[]{:S(2)}) copy-start(bf16[1,1,1,256,768]{4,3,2,1,0:T(8,128)(2,1)} %param.35) | copy-start | bytes 1179652
  39.7 40.3 %copy-start.6 = (bf16[1,1,1,256,768]{4,3,2,1,0:T(8,128)(2,1)S(1)}, bf16[1,1,1,256,768]{4,3,2,1,0:T(8,128)(2,1)}, u32[]{:S(2)}) copy-start(bf16[1,1,1,256,768]{4,3,2,1,0:T(8,128)(2,1)} %param.34) | copy-start | bytes 1179652
  97.0 8.4 %copy-start.2 = (bf16[2304,6,128]{0,2,1:T(8,128)(2,1)}, bf16[2304,6,128]{0,2,1:T(8,128)(2,1)S(1)}, u32[]{:S(2)}) copy-start(bf16[2304,6,128]{0,2,1:T(8,128)(2,1)S(1)} %copy.48) | copy-start | bytes 10616836
  116.7 9.2 %copy-start.7 = (bf16[256,768]{0,1:T(8,128)(2,1)S(1)}, bf16[256,768]{0,1:T(8,128)(2,1)}, u32[]{:S(2)}) copy-start(bf16[256,768]{0,1:T(8,128)(2,1)} %copy.43) | copy-start | bytes 1179652
  160.9 12.8 %slice-start.2 = ((s8[14155776]{0:T(1024)(128)(4,1)}), s8[4194304]{0:T(1024)(128)(4,1)S(1)}, s32[]{:S(2)}) async-start(s8[14155776]{0:T(1024)(128)(4,1)} %bitcast.228), calls=%async_computation.3 | async-start | bytes 8388608
  160.9 13.7 %slice-start.3 = ((s8[14155776]{0:T(1024)(128)(4,1)}), s8[4194304]{0:T(1024)(128)(4,1)S(1)}, s32[]{:S(2)}) async-start(s8[14155776]{0:T(1024)(128)(4,1)} %bitcast.228), calls=%async_computation.4 | async-start | bytes 8388608
  160.9 15.0 %slice-start.4 = ((s8[14155776]{0:T(1024)(128)(4,1)}), s8[4194304]{0:T(1024)(128)(4,1)S(1)}, s32[]{:S(2)}) async-start(s8[14155776]{0:T(1024)(128)(4,1)} %bitcast.228), calls=%async_computation.5 | async-start | bytes 8388608
  160.9 15.4 %slice-start.5 = ((s8[14155776]{0:T(1024)(128)(4,1)}), s8[1572864]{0:T(1024)(128)(4,1)S(1)}, s32[]{:S(2)}) async-start(s8[14155776]{0:T(1024)(128)(4,1)} %bitcast.228), calls=%async_computation.6 | async-start | bytes 3145728
  176.3 6.6 %copy-start.4 = (bf16[1,1,1,256,768]{3,4,2,1,0:T(8,128)(2,1)S(1)}, bf16[1,1,1,256,768]{3,4,2,1,0:T(8,128)(2,1)}, u32[]{:S(2)}) copy-start(bf16[1,1,1,256,768]{3,4,2,1,0:T(8,128)(2,1)} %copy.32) | copy-start | bytes 1179652
  182.9 2.9 copy-start
  221.9 10.1 %copy-start.1 = (f32[1,1,1,9,2,256,768]{6,5,3,4,2,1,0:T(8,128)S(1)}, f32[1,1,1,9,2,256,768]{6,5,3,4,2,1,0:T(8,128)}, u32[]{:S(2)}) copy-start(f32[1,1,1,9,2,256,768]{6,5,3,4,2,1,0:T(8,128)} %maximum_bitcast_fusion) | copy-start | bytes 42467332
  267.5 56.3 %collective-permute-start.5 = (bf16[3,1,2,256,768]{4,3,2,0,1:T(8,128)(2,1)S(1)}, bf16[3,1,2,256,768]{4,3,2,0,1:T(8,128)(2,1)S(1)}, u32[]{:S(2)}, u32[]{:S(2)}) collective-permute-start(bf16[3,1,2,256,768]{4,3,2,0,1:T(8,128)(2,1)S(1)} %get-tuple-element.189), channel_id=1, source_target_pairs={{4,0},{8,4},{12,8},{16,12},{20,16},{24,20},{28,24},{32,28},{36,32}... | collective-permute-start | bytes 7077896 | tf_op jit(solution)/shard_map/ppermute | solution.py:29
  274.5 68.1 %slice-start = ((s8[7077888]{0:T(1024)(128)(4,1)}), s8[4194304]{0:T(1024)(128)(4,1)S(1)}, s32[]{:S(2)}) async-start(s8[7077888]{0:T(1024)(128)(4,1)} %bitcast.226), calls=%async_computation.1 | async-start | bytes 8388608
  274.5 68.1 %slice-start.1 = ((s8[7077888]{0:T(1024)(128)(4,1)}), s8[2883584]{0:T(1024)(128)(4,1)S(1)}, s32[]{:S(2)}) async-start(s8[7077888]{0:T(1024)(128)(4,1)} %bitcast.226), calls=%async_computation.2 | async-start | bytes 5767168
  274.5 68.1 %copy-start.3 = (bf16[2304,6,128]{0,2,1:T(8,128)(2,1)S(1)}, bf16[2304,6,128]{0,2,1:T(8,128)(2,1)}, u32[]{:S(2)}) copy-start(bf16[2304,6,128]{0,2,1:T(8,128)(2,1)} %copy-done.2) | copy-start | bytes 10616836
  274.5 56.6 %collective-permute-start.4 = (bf16[3,1,2,256,768]{4,3,2,0,1:T(8,128)(2,1)S(1)}, bf16[3,1,2,256,768]{4,3,2,0,1:T(8,128)(2,1)S(1)}, u32[]{:S(2)}, u32[]{:S(2)}) collective-permute-start(bf16[3,1,2,256,768]{4,3,2,0,1:T(8,128)(2,1)S(1)} %get-tuple-element.188), channel_id=1, source_target_pairs={{0,4},{4,8},{8,12},{12,16},{16,20},{20,24},{24,28},{28,32},{32,36}... | collective-permute-start | bytes 7077896 | tf_op jit(solution)/shard_map/ppermute | solution.py:29
  336.7 7.9 %collective-permute-start.7 = (bf16[1,1,2,256,768]{4,3,2,1,0:T(8,128)(2,1)S(1)}, bf16[1,1,2,256,768]{4,3,2,1,0:T(8,128)(2,1)S(1)}, u32[]{:S(2)}, u32[]{:S(2)}) collective-permute-start(bf16[1,1,2,256,768]{4,3,2,1,0:T(8,128)(2,1)S(1)} %slice_bitcast_fusion.12), channel_id=1, source_target_pairs={{128,0},{129,1},{130,2},{131,3},{132,4},{133,5},{134,6},{135,7},{1... | collective-permute-start | bytes 2359304 | tf_op jit(solution)/shard_map/ppermute | solution.py:29
  341.2 4.2 %collective-permute-start.6 = (bf16[1,1,2,256,768]{4,3,2,1,0:T(8,128)(2,1)S(1)}, bf16[1,1,2,256,768]{4,3,2,1,0:T(8,128)(2,1)S(1)}, u32[]{:S(2)}, u32[]{:S(2)}) collective-permute-start(bf16[1,1,2,256,768]{4,3,2,1,0:T(8,128)(2,1)S(1)} %slice_bitcast_fusion.13), channel_id=1, source_target_pairs={{0,128},{1,129},{2,130},{3,131},{4,132},{5,133},{6,134},{7,135},{8... | collective-permute-start | bytes 2359304 | tf_op jit(solution)/shard_map/ppermute | solution.py:29
Sparse Core Ops, SparseCore 0:
  12.5 31.1 all-gather.1
where the time goes:
time: 361 us; the launch traced here: 355 us
  local copies, waits for them, and re-layouts  102 us (28%)
  waiting for transfers between devices  89.5 us (25%)
  other arithmetic  64.3 us (18%)
  matrix products  56.8 us (16%)
  starting transfers between devices  27.6 us (8%)
  between operations  14.7 us (4%)
    ppermute x4, waiting for transfers between devices, from_behind(): return lax.ppermute(x, axis, pairs)  55.1 us
    ppermute x2, waiting for transfers between devices, extended(): before = lax.ppermute(last, axis, up)  29.8 us
    scatter-add x8, other arithmetic, local(): spread = spread.at[1 + time_off:1 + time_off + time_tiles, 1 + row_off:1...  23.8 us
    reshape x2, local copies, waits for them, and re-layouts, query_side(): jnp.stack((grad_key.reshape(9, tile_length, feature_width), value_gradien...  18.6 us
    dot_general x1, matrix products, query_side(): jnp.einsum('hqk,qhd->khd', probs_low, grad_heads, preferred_element_type=...  17 us
    another operation x5, other arithmetic  16.7 us
    ppermute x4, starting transfers between devices, from_behind(): return lax.ppermute(x, axis, pairs)  15.1 us
    mul x1, local copies, waits for them, and re-layouts, query_side(): jnp.einsum('hqk,qhd->khd', grad_scores, query_heads, preferred_element_ty...  14 us
  transfers between devices with their start and end apart: 9, of which 7 were waited for; matrix products, arithmetic and copies ran while one was open for 7% of the time, Pallas kernels for 0%

commit v1 on v0

v1 whole, which is shorter than its diff:
```python
import jax
import jax.numpy as jnp
from jax import lax
from jax.experimental import pallas as pl
from jax.experimental.pallas import tpu as pltpu
from jax.sharding import PartitionSpec as P

HD = 128
SCALE = HD ** (-0.5)
LOG2E = 1.4426950408889634
MASKED = -1e30
FLOOR = -1e25
MESH = pl.DeviceIdType.MESH
F32 = jnp.float32
BF16 = jnp.bfloat16
SHARD = (0, 1, 3, 2)
NT = (((1,), (1,)), ((), ()))


def dot(a, b):
    return jnp.dot(a, b, preferred_element_type=F32)


def dot_nt(a, b):
    return lax.dot_general(a, b, NT, preferred_element_type=F32)


def kernel(
    heights,
    flags,
    counts,
    q_hbm,
    k_hbm,
    v_hbm,
    g_hbm,
    w_hbm,
    dq_hbm,
    dk_hbm,
    dv_hbm,
    qown,
    down,
    gall,
    wall,
    qx,
    dx,
    kb,
    vb,
    kt,
    bias,
    sbuf,
    probs,
    dprobs,
    dscaled,
    dk_acc,
    dv_acc,
    dk_low,
    dv_low,
    dq_part,
    dq_in,
    dq_out,
    st1,
    rv1,
    m_loc,
    c_row,
    c_col,
    st2,
    rv2,
    lsem,
    osem,
    g_s,
    g_r,
    q_s,
    q_r,
    sib_s,
    sib_r,
    d_s,
    d_r,
    s1_s,
    s1_r,
    s2_s,
    s2_r,
    p_s,
    p_r,
    e_s,
    e_r,
):
    t = lax.axis_index("tm")
    h = lax.axis_index("height")
    y = lax.axis_index("tensor")
    half = k_hbm.shape[1] // 2
    heads = half // HD
    tile = k_hbm.shape[0]
    grp = tile // 2
    shard = tile // 4
    lanes = 2 * grp
    sib = (1 - t, h, y)
    up, dn, up2, dn2 = h > 0, h < heights - 1, h > 1, h < heights - 2
    mine = pl.ds(pl.multiple_of(t * half, HD), half)
    other = pl.ds(pl.multiple_of((1 - t) * half, HD), half)

    def rows_of(k):
        return pl.ds(pl.multiple_of(lax.rem(y + SHARD[k], 4) * shard, shard), shard)

    def slot_of(ref, k):
        return ref.at[k // 2, pl.ds((k % 2) * shard, shard)]

    def remote(src, dst, ssem, rsem, dev):
        return pltpu.make_async_remote_copy(
            src_ref=src, dst_ref=dst, send_sem=ssem, recv_sem=rsem, device_id=dev, device_id_type=MESH
        )

    def arrived(dst, ssem, rsem):
        remote(dst, dst, ssem, rsem, sib).wait_recv()

    def sent(src, ssem, rsem):
        remote(src, src, ssem, rsem, sib).wait_send()

    q_loads = [pltpu.make_async_copy(q_hbm.at[rows_of(k)], slot_of(qown, k), lsem.at[k]) for k in range(4)]
    g_load = pltpu.make_async_copy(g_hbm, gall.at[0], lsem.at[4])
    k_load = pltpu.make_async_copy(k_hbm.at[:, mine], kb.at[t], lsem.at[5])
    v_load = pltpu.make_async_copy(v_hbm.at[:, mine], vb.at[t], lsem.at[6])
    w_load = pltpu.make_async_copy(w_hbm, wall, lsem.at[7])
    g_load.start()
    for cp in q_loads:
        cp.start()
    k_load.start()
    v_load.start()
    w_load.start()

    barrier = pltpu.get_barrier_semaphore()

    def greet(dev):
        pl.semaphore_signal(barrier, inc=1, device_id=dev, device_id_type=MESH)

    greet(sib)
    for k in (1, 2, 3):
        greet((t, h, lax.rem(y + k, 4)))

    @pl.when(up)
    def _():
        greet((0, h - 1, y))
        greet((1, h - 1, y))

    @pl.when(dn)
    def _():
        greet((0, h + 1, y))
        greet((1, h + 1, y))

    @pl.when(up2)
    def _():
        greet((t, h - 2, y))

    @pl.when(dn2)
    def _():
        greet((t, h + 2, y))

    def absent(b):
        qx[b] = jnp.zeros(qx.shape[1:], BF16)
        dx[b] = jnp.zeros(dx.shape[1:], BF16)
        dq_in[0, b] = jnp.zeros(dq_in.shape[2:], BF16)
        dq_in[1, b] = jnp.zeros(dq_in.shape[2:], BF16)

    nothing = jnp.full((8, lanes), FLOOR, F32)
    zeros = jnp.zeros((8, lanes), F32)

    def absent_stats(i):
        rv1[i] = nothing
        rv2[0, i] = zeros
        rv2[1, i] = zeros

    @pl.when(h == 0)
    def _():
        absent(0)
        absent_stats(1)
        absent_stats(2)

    @pl.when(h == heights - 1)
    def _():
        absent(2)
        absent_stats(3)
        absent_stats(4)

    @pl.when(h <= 1)
    def _():
        absent_stats(0)

    @pl.when(h >= heights - 2)
    def _():
        absent_stats(5)

    for b in range(3):
        st1[b] = zeros
        m_loc[b] = zeros
        st2[0, b] = zeros
        st2[1, b] = zeros
    dk_acc[...] = jnp.zeros(dk_acc.shape, F32)
    dv_acc[...] = jnp.zeros(dv_acc.shape, F32)

    position = lax.broadcasted_iota(jnp.int32, (tile, grp), 0)
    for b in range(3):
        hq = h + b - 1
        inside = (hq >= 0) & (hq < heights)
        hq = jnp.clip(hq, 0, heights - 1)
        for tq in range(2):
            for tk in range(2):
                flag = flags[tq, hq, 0, 3 * (tk - tq + 1) + 2 - b]
                count = jnp.where(inside & (flag > 0), counts[tk, h, 0], 0)
                bias[b, pl.ds(tk * tile, tile), pl.ds(tq * grp, grp)] = jnp.where(
                    position < count, 0.0, MASKED
                ).astype(F32)

    pl.semaphore_wait(
        barrier,
        4
        + 2 * up.astype(jnp.int32)
        + 2 * dn.astype(jnp.int32)
        + up2.astype(jnp.int32)
        + dn2.astype(jnp.int32),
    )

    g_load.wait()
    g_sends = [
        remote(gall.at[0], gall.at[2], g_s.at[0], g_r.at[1], (t, h, lax.rem(y + 1, 4))),
        remote(gall.at[0], gall.at[1], g_s.at[1], g_r.at[0], (t, h, lax.rem(y + 3, 4))),
        remote(gall.at[0], gall.at[3], g_s.at[2], g_r.at[2], (t, h, lax.rem(y + 2, 4))),
    ]
    for cp in g_sends:
        cp.start()
    for cp in q_loads:
        cp.wait()
    sib_sends = [
        remote(k_hbm.at[:, other], kb.at[t], sib_s.at[0], sib_r.at[0], sib),
        remote(v_hbm.at[:, other], vb.at[t], sib_s.at[1], sib_r.at[1], sib),
        remote(qown.at[:, :, other], qx.at[1, :, t], sib_s.at[2], sib_r.at[2], sib),
    ]
    for cp in sib_sends:
        cp.start()

    def part(c):
        return pl.ds(c * half, half)

    def q_send(c, d):
        return remote(
            qown.at[:, :, part(c)], qx.at[2 - 2 * d, :, t], q_s.at[d, c], q_r.at[1 - d, t], (c, h - 1 + 2 * d, y)
        )

    def both(fn):
        @pl.when(up)
        def _():
            fn(0)

        @pl.when(dn)
        def _():
            fn(1)

    both(lambda d: [q_send(c, d).start() for c in range(2)])
    q_copy = pltpu.make_async_copy(qown.at[:, :, mine], qx.at[1, :, t], lsem.at[8])
    q_copy.start()

    chunk = 128
    nk = 2 * tile
    chunks = nk // chunk

    def head(n):
        return pl.ds(n * HD, HD)

    def q_block(ref, b, g, n):
        return ref[b, g, :, :, head(n)].reshape(lanes, HD)

    def score_block(b):
        for g in range(2):
            for n in range(heads):
                qv = q_block(qx, b, g, n)
                top = jnp.full((8, lanes), FLOOR, F32)
                for i in range(chunks):
                    rows = pl.ds((i % (chunks // 2)) * chunk, chunk)
                    s = dot_nt(kb[i // (chunks // 2), rows, head(n)], qv) * (SCALE * LOG2E)
                    s = s + bias[b, pl.ds(i * chunk, chunk)]
                    sbuf[pl.ds(i * chunk, chunk)] = s
                    top = jnp.maximum(top, jnp.max(s.reshape(chunk // 8, 8, lanes), axis=0))
                m = jnp.max(top, axis=0, keepdims=True)
                total = jnp.zeros((8, lanes), F32)
                for i in range(chunks):
                    e = jnp.exp2(sbuf[pl.ds(i * chunk, chunk)] - m)
                    total = total + jnp.sum(e.reshape(chunk // 8, 8, lanes), axis=0)
                    probs[b, g, n, pl.ds(i * chunk, chunk)] = e.astype(BF16)
                total = jnp.sum(total, axis=0, keepdims=True)
                r = pl.ds(4 * g + n, 1)
                m_loc[b, r] = m
                st1[b, r] = m + jnp.log2(jnp.maximum(total, 1e-37))

    k_load.wait()
    v_load.wait()
    q_copy.wait()
    arrived(kb.at[1 - t], sib_s.at[0], sib_r.at[0])
    arrived(vb.at[1 - t], sib_s.at[1], sib_r.at[1])
    arrived(qx.at[1, :, 1 - t], sib_s.at[2], sib_r.at[2])
    for n in range(heads):
        kt[n] = jnp.transpose(kb[:, :, head(n)].reshape(nk, HD))
    score_block(1)

    w_load.wait()

    def d_send(i, c, d):
        src, dst = d_ref(i)
        return remote(
            src.at[:, part(c)], dst(2 - 2 * d), d_s.at[i, d, c], d_r.at[i, 1 - d, t], (c, h - 1 + 2 * d, y)
        )

    def d_region(i):
        return (0, pl.ds(0, grp)) if i == 0 else (1, pl.ds((i - 1) * shard, shard))

    def d_ref(i):
        g, rows = d_region(i)
        return down.at[g, rows], lambda b: dx.at[b, g, t, rows]

    def d_sib(i):
        g, rows = d_region(i)
        return remote(
            down.at[g, rows, other], dx.at[1, g, t, rows], d_s.at[i, 2, 0], d_r.at[i, 2, 0], sib
        )

    def project(i):
        g, rows = d_region(i)
        src = gall[pl.ds(0, 2)].reshape(grp, gall.shape[2]) if i == 0 else gall[1 + i]
        down[g, rows] = dot_nt(src, wall[...]).astype(BF16)
        both(lambda d: [d_send(i, c, d).start() for c in range(2)])
        d_sib(i).start()
        pltpu.make_async_copy(down.at[g, rows, mine], dx.at[1, g, t, rows], lsem.at[9 + i]).start()

    def d_wait(i):
        g, rows = d_region(i)
        pltpu.make_async_copy(down.at[g, rows, mine], dx.at[1, g, t, rows], lsem.at[9 + i]).wait()
        arrived(dx.at[1, g, 1 - t, rows], d_s.at[i, 2, 0], d_r.at[i, 2, 0])
        both(
            lambda d: [
                arrived(dx.at[2 * d, g, tq, rows], d_s.at[i, d, tq], d_r.at[i, d, tq]) for tq in range(2)
            ]
        )

    arrived(gall.at[1], g_s.at[0], g_r.at[0])
    project(0)
    arrived(gall.at[2], g_s.at[1], g_r.at[1])
    project(1)

    both(lambda d: [arrived(qx.at[2 * d, :, tq], q_s.at[d, tq], q_r.at[d, tq]) for tq in range(2)])

    @pl.loop(0, 2)
    def _(j):
        score_block(2 * j)

    def exchange(own, got, ssem, rsem):
        def copies():
            return (
                (up, remote(own.at[pl.ds(0, 2)], got.at[pl.ds(3, 2)], ssem.at[0], rsem.at[1], (t, h - 1, y))),
                (dn, remote(own.at[pl.ds(1, 2)], got.at[pl.ds(1, 2)], ssem.at[1], rsem.at[0], (t, h + 1, y))),
                (up2, remote(own.at[0], got.at[5], ssem.at[2], rsem.at[3], (t, h - 2, y))),
                (dn2, remote(own.at[2], got.at[0], ssem.at[3], rsem.at[2], (t, h + 2, y))),
            )

        def go():
            for cond, cp in copies():
                pl.when(cond)(cp.start)

        def finish():
            for cond, cp in copies():
                pl.when(cond)(cp.wait_send)
            for cond, dst, i in (
                (up, got.at[pl.ds(1, 2)], 0),
                (dn, got.at[pl.ds(3, 2)], 1),
                (up2, got.at[0], 2),
                (dn2, got.at[5], 3),
            ):
                pl.when(cond)(lambda dst=dst, i=i: arrived(dst, ssem.at[i], rsem.at[i]))

        return go, finish

    go1, finish1 = exchange(st1, rv1, s1_s, s1_r)
    go1()

    arrived(gall.at[3], g_s.at[2], g_r.at[2])
    project(2)

    finish1()
    for b in range(3):
        x0, x1, x2 = st1[b], rv1[2 * b], rv1[2 * b + 1]
        top = jnp.maximum(jnp.maximum(x0, x1), x2)
        lse = top + jnp.log2(jnp.exp2(x0 - top) + jnp.exp2(x1 - top) + jnp.exp2(x2 - top))
        c = jnp.exp2(m_loc[b] - lse)
        c_row[b] = c
        c_col[b] = jnp.transpose(c)

    def delta_block(b, g):
        for n in range(heads):
            col = c_col[b, :, pl.ds(4 * g + n, 1)]
            d = (q_block(dx, b, g, n).astype(F32) * col).astype(BF16)
            dscaled[b, g, n] = d
            total = jnp.zeros((8, lanes), F32)
            for i in range(chunks):
                rows = pl.ds((i % (chunks // 2)) * chunk, chunk)
                dp = dot_nt(vb[i // (chunks // 2), rows, head(n)], d)
                krows = pl.ds(i * chunk, chunk)
                dprobs[b, g, n, krows] = dp
                x = dp * probs[b, g, n, krows].astype(F32)
                total = total + jnp.sum(x.reshape(chunk // 8, 8, lanes), axis=0)
            st2[g, b, pl.ds(n, 1)] = jnp.sum(total, axis=0, keepdims=True)

    def value_block(b, g):
        for n in range(heads):
            dv_acc[n] += dot(probs[b, g, n], dscaled[b, g, n])

    def score_grad_block(b, g):
        delta = st2[g, b] + rv2[g, 2 * b] + rv2[g, 2 * b + 1]
        for n in range(heads):
            shift = delta[n : n + 1] * c_row[b, pl.ds(4 * g + n, 1)]
            ds = (probs[b, g, n].astype(F32) * (dprobs[b, g, n] - shift)).astype(BF16)
            dqt = dot(kt[n], ds) * SCALE
            dq = jnp.transpose(dqt).astype(BF16)
            dq_part[b, g, :, :, head(n)] = dq.reshape(2, grp, HD)
            dk_acc[n] += dot(ds, q_block(qx, b, g, n))

    ex2 = [exchange(st2.at[g], rv2.at[g], s2_s.at[g], s2_r.at[g]) for g in range(2)]

    def p_send(j, g, tq):
        return remote(
            dq_part.at[2 * j, g, tq],
            dq_in.at[t, 2 - 2 * j, g],
            p_s.at[g, j, tq],
            p_r.at[g, 1 - j, t],
            (tq, h - 1 + 2 * j, y),
        )

    def p_sib(g):
        return remote(dq_part.at[1, g, 1 - t], dq_in.at[t, 1, g], p_s.at[g, 2, 0], p_r.at[g, 2, 0], sib)

    def grads(g):
        @pl.loop(0, 2)
        def _(j):
            score_grad_block(2 * j, g)
            hh = h - 1 + 2 * j

            @pl.when((hh >= 0) & (hh < heights))
            def _():
                for tq in range(2):
                    p_send(j, g, tq).start()

        score_grad_block(1, g)
        p_sib(g).start()
        dq_in[t, 1, g] = dq_part[1, g, t]

    d_wait(0)

    @pl.loop(0, 3)
    def _(b):
        delta_block(b, 0)

    ex2[0][0]()

    @pl.loop(0, 3)
    def _(b):
        value_block(b, 0)

    d_wait(1)
    d_wait(2)

    @pl.loop(0, 3)
    def _(b):
        delta_block(b, 1)

    ex2[1][0]()
    ex2[0][1]()
    grads(0)

    @pl.loop(0, 3)
    def _(b):
        value_block(b, 1)

    for n in range(heads):
        dv_low[:, :, head(n)] = dv_acc[n].astype(BF16).reshape(2, tile, HD)
    dv_sib = remote(dv_low.at[1 - t], dv_hbm.at[:, mine], e_s.at[0], e_r.at[0], sib)
    dv_sib.start()
    dv_out = pltpu.make_async_copy(dv_low.at[t], dv_hbm.at[:, mine], osem.at[0])
    dv_out.start()

    ex2[1][1]()
    grads(1)

    for n in range(heads):
        dk_low[:, :, head(n)] = (dk_acc[n] * SCALE).astype(BF16).reshape(2, tile, HD)
    dk_sib = remote(dk_low.at[1 - t], dk_hbm.at[:, mine], e_s.at[1], e_r.at[1], sib)
    dk_sib.start()
    dk_out = pltpu.make_async_copy(dk_low.at[t], dk_hbm.at[:, mine], osem.at[1])
    dk_out.start()

    for g in range(2):
        arrived(dq_in.at[1 - t, 1, g], p_s.at[g, 2, 0], p_r.at[g, 2, 0])
        both(
            lambda d, g=g: [
                arrived(dq_in.at[c, 2 * d, g], p_s.at[g, d, c], p_r.at[g, d, c]) for c in range(2)
            ]
        )
        for c in range(2):
            x = dq_in[c, 0, g].astype(F32) + dq_in[c, 1, g].astype(F32) + dq_in[c, 2, g].astype(F32)
            dq_out[g, :, part(c)] = x.astype(BF16)
        for k in (2 * g, 2 * g + 1):
            pltpu.make_async_copy(slot_of(dq_out, k), dq_hbm.at[rows_of(k)], osem.at[2 + k]).start()

    for cp in g_sends + sib_sends:
        cp.wait_send()
    both(lambda d: [q_send(c, d).wait_send() for c in range(2)])
    for i in range(3):
        both(lambda d, i=i: [d_send(i, c, d).wait_send() for c in range(2)])
        d_sib(i).wait_send()
    for g in range(2):
        both(lambda d, g=g: [p_send(d, g, tq).wait_send() for tq in range(2)])
        p_sib(g).wait_send()
    dv_sib.wait_send()
    dk_sib.wait_send()
    arrived(dv_hbm.at[:, other], e_s.at[0], e_r.at[0])
    arrived(dk_hbm.at[:, other], e_s.at[1], e_r.at[1])
    dv_out.wait()
    dk_out.wait()
    for k in range(4):
        pltpu.make_async_copy(slot_of(dq_out, k), dq_hbm.at[rows_of(k)], osem.at[2 + k]).wait()


def local(queries, key_rows, value_rows, grad_output, out_weight, window_flags, valid_counts):
    tile, width = queries.shape[3:]
    model = grad_output.shape[-1]
    half = width // 2
    heads = half // HD
    grp, shard = tile // 2, tile // 4
    lanes, nk = 2 * grp, 2 * tile
    heights = lax.axis_size("height")
    shape = jax.ShapeDtypeStruct((tile, width), BF16)
    any_spec = pl.BlockSpec(memory_space=pl.ANY)
    smem = pl.BlockSpec(memory_space=pltpu.SMEM)
    dma = pltpu.SemaphoreType.DMA
    vm = pltpu.VMEM
    outs = pl.pallas_call(
        lambda *refs: kernel(heights, *refs),
        out_shape=(shape, shape, shape),
        in_specs=[smem, smem] + [any_spec] * 5,
        out_specs=(any_spec, any_spec, any_spec),
        scratch_shapes=[
            vm((2, grp, width), BF16),
            vm((2, grp, width), BF16),
            vm((4, shard, model), BF16),
            vm((width, model), BF16),
            vm((3, 2, 2, grp, half), BF16),
            vm((3, 2, 2, grp, half), BF16),
            vm((2, tile, half), BF16),
            vm((2, tile, half), BF16),
            vm((heads, HD, nk), BF16),
            vm((3, nk, lanes), F32),
            vm((nk, lanes), F32),
            vm((3, 2, heads, nk, lanes), BF16),
            vm((3, 2, heads, nk, lanes), F32),
            vm((3, 2, heads, lanes, HD), BF16),
            vm((heads, nk, HD), F32),
            vm((heads, nk, HD), F32),
            vm((2, tile, half), BF16),
            vm((2, tile, half), BF16),
            vm((3, 2, 2, grp, half), BF16),
            vm((2, 3, 2, grp, half), BF16),
            vm((2, grp, width), BF16),
            vm((3, 8, lanes), F32),
            vm((6, 8, lanes), F32),
            vm((3, 8, lanes), F32),
            vm((3, 8, lanes), F32),
            vm((3, lanes, 8), F32),
            vm((2, 3, 8, lanes), F32),
            vm((2, 6, 8, lanes), F32),
            dma((12,)),
            dma((6,)),
            dma((3,)),
            dma((3,)),
            dma((2, 2)),
            dma((2, 2)),
            dma((3,)),
            dma((3,)),
            dma((3, 3, 2)),
            dma((3, 3, 2)),
            dma((4,)),
            dma((4,)),
            dma((2, 4)),
            dma((2, 4)),
            dma((2, 3, 2)),
            dma((2, 3, 2)),
            dma((2,)),
            dma((2,)),
        ],
        compiler_params=pltpu.CompilerParams(
            collective_id=0, has_side_effects=True, vmem_limit_bytes=56 * 2**20
        ),
    )(
        window_flags,
        valid_counts,
        queries.reshape(tile, width),
        key_rows.reshape(tile, width),
        value_rows.reshape(tile, width),
        grad_output.reshape(grad_output.shape[3], model),
        out_weight,
    )
    return tuple(x.reshape(queries.shape) for x in outs)


def solution(mesh):
    wide = P("tm", "height", None, None, "tensor")
    placed = (wide, wide, wide, P("tm", "height", None, "tensor", None), P("tensor", None), P(), P())
    return jax.shard_map(local, mesh=mesh, in_specs=placed, out_specs=(wide, wide, wide), check_vma=False)
```

time: 361 us -> 60.2 us (0.17)
  the two profiles are of different devices: /device:TPU:129 before, /device:TPU:145 now
where the time goes in v1:
time: 60.2 us; the launch traced here: 59.8 us
  Pallas kernels  51.1 us (85%)
  local copies, waits for them, and re-layouts  8.08 us (13%)
  between operations  0.64 us (1%)
    pallas_call x1, Pallas kernels, local(): pl.pallas_call(lambda *refs: kernel(heights, *refs), out_shape=(shape, sh...  51.1 us
    unnamed x5, local copies, waits for them, and re-layouts  8.08 us

profile of v1, /device:TPU:145, one launch (start us, length us, event | category | flops | bytes accessed | tf_op | source)
XLA Modules:
  0.0 59.8 jit_solution(11709047855715083935)
XLA Ops:
  0.6 1.4 %copy.10.refs_0_ = s32[2,32,1,9]{3,2,1,0:T(1,128)} copy(s32[2,32,1,9]{1,2,3,0:T(1,128)} %param.12) | data formatting | bytes 4608 | tf_op args[5]
  2.0 1.4 %copy.11.refs_1_ = s32[2,32,1]{2,1,0:T(8,128)} copy(s32[2,32,1]{1,2,0:T(1,128)} %param.13) | data formatting | bytes 512 | tf_op args[6]
  3.4 51.1 %shard_map.94 = (bf16[256,768]{1,0:T(8,128)(2,1)}, bf16[256,768]{1,0:T(8,128)(2,1)}, bf16[256,768]{1,0:T(8,128)(2,1)}) custom-call(s32[2,32,1,9]{3,2,1,0:T(1,128)} %copy.10.refs_0_, s32[2,32,1]{2,1,0:T(8,128)} %copy.11.refs_1_, bf16[256,768]{1,0:T(8,128)(2,1)} %bitcast.7, bf16[256,768]{1,0:T(8,128)(2,1)} %bitcast.8, bf16[256,768]{1,0:T(8,128)(2,1)} %bitcast.9, ...), custom_call_target="tpu_custom_call" | custom-call | tf_op jit(solution)/shard_map/pallas_call | solution.py:540
  54.5 1.8 %copy.15 = bf16[1,1,1,256,768]{4,3,2,1,0:T(8,128)(2,1)} copy(bf16[1,1,1,256,768]{4,3,2,1,0:T(8,128)(2,1)} %bitcast.13) | data formatting | bytes 786432
  56.3 1.8 %copy.16 = bf16[1,1,1,256,768]{4,3,2,1,0:T(8,128)(2,1)} copy(bf16[1,1,1,256,768]{4,3,2,1,0:T(8,128)(2,1)} %bitcast.12) | data formatting | bytes 786432
  58.0 1.8 %copy.17 = bf16[1,1,1,256,768]{4,3,2,1,0:T(8,128)(2,1)} copy(bf16[1,1,1,256,768]{4,3,2,1,0:T(8,128)(2,1)} %bitcast.11) | data formatting | bytes 786432

commit v2 on v1

--- a/solution.py
+++ b/solution.py
@@ -27,8 +27,8 @@
 
 def kernel(
     heights,
-    flags,
-    counts,
+    f_hbm,
+    n_hbm,
     q_hbm,
     k_hbm,
     v_hbm,
@@ -37,6 +37,8 @@
     dq_hbm,
     dk_hbm,
     dv_hbm,
+    flags,
+    counts,
     qown,
     down,
     gall,
@@ -120,6 +122,10 @@
     k_load = pltpu.make_async_copy(k_hbm.at[:, mine], kb.at[t], lsem.at[5])
     v_load = pltpu.make_async_copy(v_hbm.at[:, mine], vb.at[t], lsem.at[6])
     w_load = pltpu.make_async_copy(w_hbm, wall, lsem.at[7])
+    f_load = pltpu.make_async_copy(f_hbm, flags, lsem.at[12])
+    n_load = pltpu.make_async_copy(n_hbm, counts, lsem.at[13])
+    f_load.start()
+    n_load.start()
     g_load.start()
     for cp in q_loads:
         cp.start()
@@ -196,15 +202,22 @@
     dk_acc[...] = jnp.zeros(dk_acc.shape, F32)
     dv_acc[...] = jnp.zeros(dv_acc.shape, F32)
 
-    position = lax.broadcasted_iota(jnp.int32, (tile, grp), 0)
+    f_load.wait()
+    n_load.wait()
+    position = lax.broadcasted_iota(jnp.int32, (tile, grp), 0).astype(F32)
+    lane = lax.broadcasted_iota(jnp.int32, (1, heights), 1)
+
+    def at_height(row, i):
+        return jnp.sum(jnp.where(lane == i, row.astype(F32), 0.0), axis=1, keepdims=True)
+
     for b in range(3):
         hq = h + b - 1
         inside = (hq >= 0) & (hq < heights)
         hq = jnp.clip(hq, 0, heights - 1)
         for tq in range(2):
             for tk in range(2):
-                flag = flags[tq, hq, 0, 3 * (tk - tq + 1) + 2 - b]
-                count = jnp.where(inside & (flag > 0), counts[tk, h, 0], 0)
+                flag = at_height(flags[tq, 3 * (tk - tq + 1) + 2 - b], hq)
+                count = jnp.where(inside & (flag > 0.0), at_height(counts[tk], h), 0.0)
                 bias[b, pl.ds(tk * tile, tile), pl.ds(tq * grp, grp)] = jnp.where(
                     position < count, 0.0, MASKED
                 ).astype(F32)
@@ -524,6 +537,12 @@
         pltpu.make_async_copy(slot_of(dq_out, k), dq_hbm.at[rows_of(k)], osem.at[2 + k]).wait()
 
 
+def hand_over(a, b, c, x, y, z):
+    x[...] = a[...]
+    y[...] = b[...]
+    z[...] = c[...]
+
+
 def local(queries, key_rows, value_rows, grad_output, out_weight, window_flags, valid_counts):
     tile, width = queries.shape[3:]
     model = grad_output.shape[-1]
@@ -534,15 +553,16 @@
     heights = lax.axis_size("height")
     shape = jax.ShapeDtypeStruct((tile, width), BF16)
     any_spec = pl.BlockSpec(memory_space=pl.ANY)
-    smem = pl.BlockSpec(memory_space=pltpu.SMEM)
     dma = pltpu.SemaphoreType.DMA
     vm = pltpu.VMEM
     outs = pl.pallas_call(
         lambda *refs: kernel(heights, *refs),
         out_shape=(shape, shape, shape),
-        in_specs=[smem, smem] + [any_spec] * 5,
+        in_specs=[any_spec] * 7,
         out_specs=(any_spec, any_spec, any_spec),
         scratch_shapes=[
+            vm((2, 9, 1, heights), jnp.int32),
+            vm((2, 1, heights), jnp.int32),
             vm((2, grp, width), BF16),
             vm((2, grp, width), BF16),
             vm((4, shard, model), BF16),
@@ -571,7 +591,7 @@
             vm((3, lanes, 8), F32),
             vm((2, 3, 8, lanes), F32),
             vm((2, 6, 8, lanes), F32),
-            dma((12,)),
+            dma((14,)),
             dma((6,)),
             dma((3,)),
             dma((3,)),
@@ -594,14 +614,15 @@
             collective_id=0, has_side_effects=True, vmem_limit_bytes=56 * 2**20
         ),
     )(
-        window_flags,
-        valid_counts,
+        window_flags.transpose(0, 3, 2, 1),
+        valid_counts.transpose(0, 2, 1),
         queries.reshape(tile, width),
         key_rows.reshape(tile, width),
         value_rows.reshape(tile, width),
         grad_output.reshape(grad_output.shape[3], model),
         out_weight,
     )
+    outs = pl.pallas_call(hand_over, out_shape=(shape, shape, shape))(*outs)
     return tuple(x.reshape(queries.shape) for x in outs)
 
 

time: 60.2 us -> 52.9 us (0.88)
  local copies, waits for them, and re-layouts: 8.08 us -> 0 us
  Pallas kernels: 51.1 us -> 52.1 us
    unnamed x5 -> x0, local copies, waits for them, and re-layouts: 8.08 us -> none
    pallas_call x0 -> x1, Pallas kernels: none -> 2.27 us  [local(): outs = pl.pallas_call(hand_over, out_shape=(shape, shape, shape))(*outs)]
    pallas_call x1, Pallas kernels: 51.1 us -> 49.8 us  [local(): pl.pallas_call(lambda *refs: kernel(heights, *refs), out_shape=(shape, sh...]
where the time goes in v2:
time: 52.9 us; the launch traced here: 52.7 us
  Pallas kernels  52.1 us (98%)
  between operations  0.64 us (1%)
    pallas_call x1, Pallas kernels, local(): pl.pallas_call(lambda *refs: kernel(heights, *refs), out_shape=(shape, sh...  49.8 us
    pallas_call x1, Pallas kernels, local(): outs = pl.pallas_call(hand_over, out_shape=(shape, shape, shape))(*outs)  2.27 us

profile of v2, /device:TPU:145, one launch (start us, length us, event | category | flops | bytes accessed | tf_op | source)
XLA Modules:
  0.0 52.7 jit_solution(12335915963938923923)
XLA Ops:
  0.6 49.8 %shard_map.94 = (bf16[256,768]{1,0:T(8,128)(2,1)}, bf16[256,768]{1,0:T(8,128)(2,1)}, bf16[256,768]{1,0:T(8,128)(2,1)}) custom-call(s32[2,9,1,32]{3,2,1,0:T(1,128)} %bitcast.15, s32[2,1,32]{2,1,0:T(1,128)} %bitcast.16, bf16[256,768]{1,0:T(8,128)(2,1)} %bitcast.11, bf16[256,768]{1,0:T(8,128)(2,1)} %bitcast.12, bf16[256,768]{1,0:T(8,128)(2,1)} %bitcast.13, ...), custom_call_target="tpu_custom_call" | custom-call | tf_op jit(solution)/shard_map/pallas_call | solution.py:558
  50.5 2.3 %shard_map.95 = (bf16[256,768]{1,0:T(8,128)(2,1)}, bf16[256,768]{1,0:T(8,128)(2,1)}, bf16[256,768]{1,0:T(8,128)(2,1)}) custom-call(bf16[256,768]{1,0:T(8,128)(2,1)} %get-tuple-element.9.a, bf16[256,768]{1,0:T(8,128)(2,1)} %get-tuple-element.10.b, bf16[256,768]{1,0:T(8,128)(2,1)} %get-tuple-element.11.c), custom_call_target="tpu_custom_call" | custom-call | tf_op jit(solution)/shard_map/pallas_call | solution.py:625

commit v3 on v2

--- a/solution.py
+++ b/solution.py
@@ -34,7 +34,7 @@
     v_hbm,
     g_hbm,
     w_hbm,
-    dq_hbm,
+    parts,
     dk_hbm,
     dv_hbm,
     flags,
@@ -58,8 +58,6 @@
     dk_low,
     dv_low,
     dq_part,
-    dq_in,
-    dq_out,
     st1,
     rv1,
     m_loc,
@@ -122,8 +120,8 @@
     k_load = pltpu.make_async_copy(k_hbm.at[:, mine], kb.at[t], lsem.at[5])
     v_load = pltpu.make_async_copy(v_hbm.at[:, mine], vb.at[t], lsem.at[6])
     w_load = pltpu.make_async_copy(w_hbm, wall, lsem.at[7])
-    f_load = pltpu.make_async_copy(f_hbm, flags, lsem.at[12])
-    n_load = pltpu.make_async_copy(n_hbm, counts, lsem.at[13])
+    f_load = pltpu.make_async_copy(f_hbm, flags, lsem.at[13])
+    n_load = pltpu.make_async_copy(n_hbm, counts, lsem.at[14])
     f_load.start()
     n_load.start()
     g_load.start()
@@ -160,11 +158,13 @@
     def _():
         greet((t, h + 2, y))
 
+    def zero_part(b):
+        return pltpu.make_async_copy(dx.at[b], parts.at[:, b], osem.at[2])
+
     def absent(b):
         qx[b] = jnp.zeros(qx.shape[1:], BF16)
         dx[b] = jnp.zeros(dx.shape[1:], BF16)
-        dq_in[0, b] = jnp.zeros(dq_in.shape[2:], BF16)
-        dq_in[1, b] = jnp.zeros(dq_in.shape[2:], BF16)
+        zero_part(b).start()
 
     nothing = jnp.full((8, lanes), FLOOR, F32)
     zeros = jnp.zeros((8, lanes), F32)
@@ -232,10 +232,17 @@
     )
 
     g_load.wait()
+    ahead, behind = (t, h, lax.rem(y + 1, 4)), (t, h, lax.rem(y + 3, 4))
+    first, second = pl.ds(0, shard // 2), pl.ds(shard // 2, shard // 2)
     g_sends = [
-        remote(gall.at[0], gall.at[2], g_s.at[0], g_r.at[1], (t, h, lax.rem(y + 1, 4))),
-        remote(gall.at[0], gall.at[1], g_s.at[1], g_r.at[0], (t, h, lax.rem(y + 3, 4))),
-        remote(gall.at[0], gall.at[3], g_s.at[2], g_r.at[2], (t, h, lax.rem(y + 2, 4))),
+        remote(gall.at[0, first], gall.at[2, first], g_s.at[0], g_r.at[0], ahead),
+        remote(gall.at[0, second], gall.at[1, second], g_s.at[1], g_r.at[1], behind),
+        remote(gall.at[0, second], gall.at[2, second], g_s.at[2], g_r.at[2], ahead),
+        remote(gall.at[0, first], gall.at[1, first], g_s.at[3], g_r.at[3], behind),
+    ]
+    g_relays = [
+        remote(gall.at[2, first], gall.at[3, first], g_s.at[4], g_r.at[4], ahead),
+        remote(gall.at[1, second], gall.at[3, second], g_s.at[5], g_r.at[5], behind),
     ]
     for cp in g_sends:
         cp.start()
@@ -321,7 +328,7 @@
         )
 
     def d_region(i):
-        return (0, pl.ds(0, grp)) if i == 0 else (1, pl.ds((i - 1) * shard, shard))
+        return i // 2, pl.ds((i % 2) * shard, shard)
 
     def d_ref(i):
         g, rows = d_region(i)
@@ -335,8 +342,7 @@
 
     def project(i):
         g, rows = d_region(i)
-        src = gall[pl.ds(0, 2)].reshape(grp, gall.shape[2]) if i == 0 else gall[1 + i]
-        down[g, rows] = dot_nt(src, wall[...]).astype(BF16)
+        down[g, rows] = dot_nt(gall[i], wall[...]).astype(BF16)
         both(lambda d: [d_send(i, c, d).start() for c in range(2)])
         d_sib(i).start()
         pltpu.make_async_copy(down.at[g, rows, mine], dx.at[1, g, t, rows], lsem.at[9 + i]).start()
@@ -351,10 +357,15 @@
             ]
         )
 
-    arrived(gall.at[1], g_s.at[0], g_r.at[0])
     project(0)
-    arrived(gall.at[2], g_s.at[1], g_r.at[1])
+    arrived(gall.at[2, first], g_s.at[0], g_r.at[0])
+    g_relays[0].start()
+    arrived(gall.at[1, second], g_s.at[1], g_r.at[1])
+    g_relays[1].start()
+    arrived(gall.at[1, first], g_s.at[3], g_r.at[3])
     project(1)
+    arrived(gall.at[2, second], g_s.at[2], g_r.at[2])
+    project(2)
 
     both(lambda d: [arrived(qx.at[2 * d, :, tq], q_s.at[d, tq], q_r.at[d, tq]) for tq in range(2)])
 
@@ -391,8 +402,9 @@
     go1, finish1 = exchange(st1, rv1, s1_s, s1_r)
     go1()
 
-    arrived(gall.at[3], g_s.at[2], g_r.at[2])
-    project(2)
+    arrived(gall.at[3, first], g_s.at[4], g_r.at[4])
+    arrived(gall.at[3, second], g_s.at[5], g_r.at[5])
+    project(3)
 
     finish1()
     for b in range(3):
@@ -437,14 +449,17 @@
     def p_send(j, g, tq):
         return remote(
             dq_part.at[2 * j, g, tq],
-            dq_in.at[t, 2 - 2 * j, g],
+            parts.at[t, 2 - 2 * j, g],
             p_s.at[g, j, tq],
             p_r.at[g, 1 - j, t],
             (tq, h - 1 + 2 * j, y),
         )
 
     def p_sib(g):
-        return remote(dq_part.at[1, g, 1 - t], dq_in.at[t, 1, g], p_s.at[g, 2, 0], p_r.at[g, 2, 0], sib)
+        return remote(dq_part.at[1, g, 1 - t], parts.at[t, 1, g], p_s.at[g, 2, 0], p_r.at[g, 2, 0], sib)
+
+    def p_own(g):
+        return pltpu.make_async_copy(dq_part.at[1, g, t], parts.at[t, 1, g], osem.at[3 + g])
 
     def grads(g):
         @pl.loop(0, 2)
@@ -459,9 +474,10 @@
 
         score_grad_block(1, g)
         p_sib(g).start()
-        dq_in[t, 1, g] = dq_part[1, g, t]
+        p_own(g).start()
 
     d_wait(0)
+    d_wait(1)
 
     @pl.loop(0, 3)
     def _(b):
@@ -473,8 +489,8 @@
     def _(b):
         value_block(b, 0)
 
-    d_wait(1)
     d_wait(2)
+    d_wait(3)
 
     @pl.loop(0, 3)
     def _(b):
@@ -506,22 +522,20 @@
     dk_out.start()
 
     for g in range(2):
-        arrived(dq_in.at[1 - t, 1, g], p_s.at[g, 2, 0], p_r.at[g, 2, 0])
+        p_own(g).wait()
+        arrived(parts.at[1 - t, 1, g], p_s.at[g, 2, 0], p_r.at[g, 2, 0])
         both(
             lambda d, g=g: [
-                arrived(dq_in.at[c, 2 * d, g], p_s.at[g, d, c], p_r.at[g, d, c]) for c in range(2)
+                arrived(parts.at[c, 2 * d, g], p_s.at[g, d, c], p_r.at[g, d, c]) for c in range(2)
             ]
         )
-        for c in range(2):
-            x = dq_in[c, 0, g].astype(F32) + dq_in[c, 1, g].astype(F32) + dq_in[c, 2, g].astype(F32)
-            dq_out[g, :, part(c)] = x.astype(BF16)
-        for k in (2 * g, 2 * g + 1):
-            pltpu.make_async_copy(slot_of(dq_out, k), dq_hbm.at[rows_of(k)], osem.at[2 + k]).start()
-
-    for cp in g_sends + sib_sends:
+    pl.when(h == 0)(zero_part(0).wait)
+    pl.when(h == heights - 1)(zero_part(2).wait)
+
+    for cp in g_sends + g_relays + sib_sends:
         cp.wait_send()
     both(lambda d: [q_send(c, d).wait_send() for c in range(2)])
-    for i in range(3):
+    for i in range(4):
         both(lambda d, i=i: [d_send(i, c, d).wait_send() for c in range(2)])
         d_sib(i).wait_send()
     for g in range(2):
@@ -533,14 +547,43 @@
     arrived(dk_hbm.at[:, other], e_s.at[1], e_r.at[1])
     dv_out.wait()
     dk_out.wait()
+
+
+def finish(parts, dk, dv, dq_hbm, dk_hbm, dv_hbm, buf, dk_buf, dv_buf, dq_out, sem):
+    y = lax.axis_index("tensor")
+    grp, half = buf.shape[3:]
+    shard = grp // 2
+    loads = [
+        pltpu.make_async_copy(parts.at[:, :, 0], buf.at[0], sem.at[0]),
+        pltpu.make_async_copy(parts.at[:, :, 1], buf.at[1], sem.at[1]),
+        pltpu.make_async_copy(dk, dk_buf, sem.at[2]),
+        pltpu.make_async_copy(dv, dv_buf, sem.at[3]),
+    ]
+    stores = [
+        pltpu.make_async_copy(dk_buf, dk_hbm, sem.at[4]),
+        pltpu.make_async_copy(dv_buf, dv_hbm, sem.at[5]),
+    ]
     for k in range(4):
-        pltpu.make_async_copy(slot_of(dq_out, k), dq_hbm.at[rows_of(k)], osem.at[2 + k]).wait()
-
-
-def hand_over(a, b, c, x, y, z):
-    x[...] = a[...]
-    y[...] = b[...]
-    z[...] = c[...]
+        rows = pl.ds(pl.multiple_of(lax.rem(y + SHARD[k], 4) * shard, shard), shard)
+        stores.append(
+            pltpu.make_async_copy(
+                dq_out.at[k // 2, pl.ds((k % 2) * shard, shard)], dq_hbm.at[rows], sem.at[6 + k]
+            )
+        )
+    for cp in loads:
+        cp.start()
+    for g in range(2):
+        loads[g].wait()
+        for c in range(2):
+            x = buf[g, c, 0].astype(F32) + buf[g, c, 1].astype(F32) + buf[g, c, 2].astype(F32)
+            dq_out[g, :, pl.ds(c * half, half)] = x.astype(BF16)
+        stores[2 + 2 * g].start()
+        stores[3 + 2 * g].start()
+    for i in range(2):
+        loads[2 + i].wait()
+        stores[i].start()
+    for cp in stores:
+        cp.wait()
 
 
 def local(queries, key_rows, value_rows, grad_output, out_weight, window_flags, valid_counts):
@@ -552,12 +595,13 @@
     lanes, nk = 2 * grp, 2 * tile
     heights = lax.axis_size("height")
     shape = jax.ShapeDtypeStruct((tile, width), BF16)
+    parts_shape = jax.ShapeDtypeStruct((2, 3, 2, grp, half), BF16)
     any_spec = pl.BlockSpec(memory_space=pl.ANY)
     dma = pltpu.SemaphoreType.DMA
     vm = pltpu.VMEM
     outs = pl.pallas_call(
         lambda *refs: kernel(heights, *refs),
-        out_shape=(shape, shape, shape),
+        out_shape=(parts_shape, shape, shape),
         in_specs=[any_spec] * 7,
         out_specs=(any_spec, any_spec, any_spec),
         scratch_shapes=[
@@ -582,8 +626,6 @@
             vm((2, tile, half), BF16),
             vm((2, tile, half), BF16),
             vm((3, 2, 2, grp, half), BF16),
-            vm((2, 3, 2, grp, half), BF16),
-            vm((2, grp, width), BF16),
             vm((3, 8, lanes), F32),
             vm((6, 8, lanes), F32),
             vm((3, 8, lanes), F32),
@@ -591,16 +633,16 @@
             vm((3, lanes, 8), F32),
             vm((2, 3, 8, lanes), F32),
             vm((2, 6, 8, lanes), F32),
-            dma((14,)),
+            dma((15,)),
             dma((6,)),
-            dma((3,)),
-            dma((3,)),
+            dma((6,)),
+            dma((6,)),
             dma((2, 2)),
             dma((2, 2)),
             dma((3,)),
             dma((3,)),
-            dma((3, 3, 2)),
-            dma((3, 3, 2)),
+            dma((4, 3, 2)),
+            dma((4, 3, 2)),
             dma((4,)),
             dma((4,)),
             dma((2, 4)),
@@ -622,7 +664,19 @@
         grad_output.reshape(grad_output.shape[3], model),
         out_weight,
     )
-    outs = pl.pallas_call(hand_over, out_shape=(shape, shape, shape))(*outs)
+    outs = pl.pallas_call(
+        finish,
+        out_shape=(shape, shape, shape),
+        in_specs=[any_spec] * 3,
+        out_specs=(any_spec,) * 3,
+        scratch_shapes=[
+            vm((2, 2, 3, grp, half), BF16),
+            vm((tile, width), BF16),
+            vm((tile, width), BF16),
+            vm((2, grp, width), BF16),
+            dma((10,)),
+        ],
+    )(*outs)
     return tuple(x.reshape(queries.shape) for x in outs)
 
 

time: 52.9 us -> 48.6 us (0.919)
  the two profiles are of different devices: /device:TPU:145 before, /device:TPU:129 now
where the time goes in v3:
time: 48.6 us; the launch traced here: 48.4 us
  Pallas kernels  47.8 us (98%)
  between operations  0.64 us (1%)
    pallas_call x1, Pallas kernels, local(): pl.pallas_call(lambda *refs: kernel(heights, *refs), out_shape=(parts_sha...  45.4 us
    pallas_call x1, Pallas kernels, local(): pl.pallas_call(finish, out_shape=(shape, shape, shape), in_specs=[any_spe...  2.35 us

profile of v3, /device:TPU:129, one launch (start us, length us, event | category | flops | bytes accessed | tf_op | source)
XLA Modules:
  0.0 48.4 jit_solution(13644132651229999335)
XLA Ops:
  0.6 45.4 %shard_map.94 = (bf16[2,3,2,128,384]{4,3,2,1,0:T(8,128)(2,1)}, bf16[256,768]{1,0:T(8,128)(2,1)}, bf16[256,768]{1,0:T(8,128)(2,1)}) custom-call(s32[2,9,1,32]{3,2,1,0:T(1,128)} %bitcast.15, s32[2,1,32]{2,1,0:T(1,128)} %bitcast.16, bf16[256,768]{1,0:T(8,128)(2,1)} %bitcast.11, bf16[256,768]{1,0:T(8,128)(2,1)} %bitcast.12, bf16[256,768]{1,0:T(8,128)(2,1)} %bitcast.13, ...), custom_call_target="tpu_custom_call" | custom-call | tf_op jit(solution)/shard_map/pallas_call | solution.py:602
  46.1 2.4 %shard_map.95 = (bf16[256,768]{1,0:T(8,128)(2,1)}, bf16[256,768]{1,0:T(8,128)(2,1)}, bf16[256,768]{1,0:T(8,128)(2,1)}) custom-call(bf16[2,3,2,128,384]{4,3,2,1,0:T(8,128)(2,1)} %get-tuple-element.9.parts, bf16[256,768]{1,0:T(8,128)(2,1)} %get-tuple-element.10.dk, bf16[256,768]{1,0:T(8,128)(2,1)} %get-tuple-element.11.dv), custom_call_target="tpu_custom_call" | custom-call | tf_op jit(solution)/shard_map/pallas_call | solution.py:667

commit v4 on v3

v4 whole, which is shorter than its diff:
```python
import jax
import jax.numpy as jnp
from jax import lax
from jax.experimental import pallas as pl
from jax.experimental.pallas import tpu as pltpu
from jax.sharding import PartitionSpec as P

HD = 128
SCALE = HD ** (-0.5)
LOG2E = 1.4426950408889634
MASKED = -1e30
FLOOR = -1e25
MESH = pl.DeviceIdType.MESH
F32 = jnp.float32
BF16 = jnp.bfloat16
SHARD = (0, 1, 3, 2)
NT = (((1,), (1,)), ((), ()))


def dot(a, b):
    return jnp.dot(a, b, preferred_element_type=F32)


def dot_nt(a, b):
    return lax.dot_general(a, b, NT, preferred_element_type=F32)


def kernel(
    heights,
    f_hbm,
    n_hbm,
    q_hbm,
    k_hbm,
    v_hbm,
    g_hbm,
    w_hbm,
    parts,
    dk_hbm,
    dv_hbm,
    flags,
    counts,
    qown,
    down,
    gall,
    wall,
    qx,
    dx,
    kb,
    vb,
    kt,
    bias,
    sbuf,
    probs,
    dprobs,
    dscores,
    dk_acc,
    dv_acc,
    dk_low,
    dv_low,
    dq_part,
    st,
    rv,
    loc,
    row,
    col,
    lsem,
    osem,
    g_s,
    g_r,
    q_s,
    q_r,
    sib_s,
    sib_r,
    d_s,
    d_r,
    st_s,
    st_r,
    p_s,
    p_r,
    e_s,
    e_r,
):
    t = lax.axis_index("tm")
    h = lax.axis_index("height")
    y = lax.axis_index("tensor")
    half = k_hbm.shape[1] // 2
    heads = half // HD
    tile = k_hbm.shape[0]
    shard = tile // 4
    pair = 2 * shard
    lanes = 2 * pair
    sib = (1 - t, h, y)
    up, dn, up2, dn2 = h > 0, h < heights - 1, h > 1, h < heights - 2
    mine = pl.ds(pl.multiple_of(t * half, HD), half)
    other = pl.ds(pl.multiple_of((1 - t) * half, HD), half)

    def rows_of(k):
        return pl.ds(pl.multiple_of(lax.rem(y + SHARD[k], 4) * shard, shard), shard)

    def remote(src, dst, ssem, rsem, dev):
        return pltpu.make_async_remote_copy(
            src_ref=src, dst_ref=dst, send_sem=ssem, recv_sem=rsem, device_id=dev, device_id_type=MESH
        )

    def arrived(dst, ssem, rsem):
        remote(dst, dst, ssem, rsem, sib).wait_recv()

    def sent(src, ssem, rsem):
        remote(src, src, ssem, rsem, sib).wait_send()

    q_loads = [pltpu.make_async_copy(q_hbm.at[rows_of(k)], qown.at[k], lsem.at[k]) for k in range(4)]
    g_load = pltpu.make_async_copy(g_hbm, gall.at[0], lsem.at[4])
    k_load = pltpu.make_async_copy(k_hbm.at[:, mine], kb.at[t], lsem.at[5])
    v_load = pltpu.make_async_copy(v_hbm.at[:, mine], vb.at[t], lsem.at[6])
    w_load = pltpu.make_async_copy(w_hbm, wall, lsem.at[7])
    f_load = pltpu.make_async_copy(f_hbm, flags, lsem.at[13])
    n_load = pltpu.make_async_copy(n_hbm, counts, lsem.at[14])
    f_load.start()
    n_load.start()
    g_load.start()
    for cp in q_loads:
        cp.start()
    k_load.start()
    v_load.start()
    w_load.start()

    barrier = pltpu.get_barrier_semaphore()

    def greet(dev):
        pl.semaphore_signal(barrier, inc=1, device_id=dev, device_id_type=MESH)

    greet(sib)
    for k in (1, 2, 3):
        greet((t, h, lax.rem(y + k, 4)))

    @pl.when(up)
    def _():
        greet((0, h - 1, y))
        greet((1, h - 1, y))

    @pl.when(dn)
    def _():
        greet((0, h + 1, y))
        greet((1, h + 1, y))

    @pl.when(up2)
    def _():
        greet((t, h - 2, y))

    @pl.when(dn2)
    def _():
        greet((t, h + 2, y))

    def zero_part(b, c):
        return pltpu.make_async_copy(dx.at[pl.ds(0, 4), b // 2, c], parts.at[c, b], osem.at[2 + c])

    def absent(b):
        for k in range(4):
            qx[k, b // 2] = jnp.zeros(qx.shape[2:], BF16)
            dx[k, b // 2] = jnp.zeros(dx.shape[2:], BF16)
        for c in range(2):
            zero_part(b, c).start()

    sub = lax.broadcasted_iota(jnp.int32, (8, pair), 0)
    nothing = jnp.where(sub < 4, FLOOR, 0.0).astype(F32)
    zeros = jnp.zeros((8, pair), F32)

    def absent_stats(i):
        for k in range(4):
            rv[k, i] = nothing

    @pl.when(h == 0)
    def _():
        absent(0)
        absent_stats(1)
        absent_stats(2)

    @pl.when(h == heights - 1)
    def _():
        absent(2)
        absent_stats(3)
        absent_stats(4)

    @pl.when(h <= 1)
    def _():
        absent_stats(0)

    @pl.when(h >= heights - 2)
    def _():
        absent_stats(5)

    for k in range(4):
        for b in range(3):
            st[k, b] = zeros
            loc[k, b] = zeros
    dk_acc[...] = jnp.zeros(dk_acc.shape, F32)
    dv_acc[...] = jnp.zeros(dv_acc.shape, F32)

    f_load.wait()
    n_load.wait()
    position = lax.broadcasted_iota(jnp.int32, (tile, pair), 0).astype(F32)
    late = lax.broadcasted_iota(jnp.int32, (1, pair), 1) >= shard
    lane = lax.broadcasted_iota(jnp.int32, (1, heights), 1)

    def at_height(values, i):
        return jnp.sum(jnp.where(lane == i, values.astype(F32), 0.0), axis=1, keepdims=True)

    for b in range(3):
        hq = h + b - 1
        inside = (hq >= 0) & (hq < heights)
        hq = jnp.clip(hq, 0, heights - 1)
        for tk in range(2):
            count = []
            for tq in range(2):
                flag = at_height(flags[tq, 3 * (tk - tq + 1) + 2 - b], hq)
                count.append(jnp.where(inside & (flag > 0.0), at_height(counts[tk], h), 0.0))
            limit = jnp.where(late, count[1], count[0])
            value = jnp.where(position < limit, 0.0, MASKED).astype(F32)
            krows = pl.ds(tk * tile, tile)
            if b == 1:
                bias[1, krows, pl.ds(0, pair)] = value
                bias[1, krows, pl.ds(pair, pair)] = value
            else:
                bias[0, krows, pl.ds((b // 2) * pair, pair)] = value

    pl.semaphore_wait(
        barrier,
        4
        + 2 * up.astype(jnp.int32)
        + 2 * dn.astype(jnp.int32)
        + up2.astype(jnp.int32)
        + dn2.astype(jnp.int32),
    )

    g_load.wait()
    ahead, behind = (t, h, lax.rem(y + 1, 4)), (t, h, lax.rem(y + 3, 4))
    first, second = pl.ds(0, shard // 2), pl.ds(shard // 2, shard // 2)
    g_sends = [
        remote(gall.at[0, first], gall.at[2, first], g_s.at[0], g_r.at[0], ahead),
        remote(gall.at[0, second], gall.at[1, second], g_s.at[1], g_r.at[1], behind),
        remote(gall.at[0, second], gall.at[2, second], g_s.at[2], g_r.at[2], ahead),
        remote(gall.at[0, first], gall.at[1, first], g_s.at[3], g_r.at[3], behind),
    ]
    g_relays = [
        remote(gall.at[2, first], gall.at[3, first], g_s.at[4], g_r.at[4], ahead),
        remote(gall.at[1, second], gall.at[3, second], g_s.at[5], g_r.at[5], behind),
    ]
    for cp in g_sends:
        cp.start()
    for cp in q_loads:
        cp.wait()
    sib_sends = [
        remote(k_hbm.at[:, other], kb.at[t], sib_s.at[0], sib_r.at[0], sib),
        remote(v_hbm.at[:, other], vb.at[t], sib_s.at[1], sib_r.at[1], sib),
        remote(qown.at[pl.ds(0, 2), :, other], qx.at[4, :, t], sib_s.at[2], sib_r.at[2], sib),
        remote(qown.at[pl.ds(2, 2), :, other], qx.at[5, :, t], sib_s.at[3], sib_r.at[3], sib),
    ]
    for cp in sib_sends:
        cp.start()

    def part(c):
        return pl.ds(c * half, half)

    def q_send(c, d):
        return remote(
            qown.at[:, :, part(c)],
            qx.at[pl.ds(0, 4), 1 - d, t],
            q_s.at[d, c],
            q_r.at[1 - d, t],
            (c, h - 1 + 2 * d, y),
        )

    def both(fn):
        @pl.when(up)
        def _():
            fn(0)

        @pl.when(dn)
        def _():
            fn(1)

    both(lambda d: [q_send(c, d).start() for c in range(2)])
    q_copies = [
        pltpu.make_async_copy(qown.at[pl.ds(2 * g, 2), :, mine], qx.at[4 + g, :, t], lsem.at[(8, 15)[g]])
        for g in range(2)
    ]
    for cp in q_copies:
        cp.start()

    chunk = 128
    nk = 2 * tile
    chunks = nk // chunk

    def head(n):
        return pl.ds(n * HD, HD)

    def rows_block(ref, u, n):
        return ref[u, :, :, :, head(n)].reshape(lanes, HD)

    def halo(s):
        return ((s, 0), (s, 2))

    def own(g):
        return ((2 * g, 1), (2 * g + 1, 1))

    def put(ref, places, r, value):
        for i, (s, b) in enumerate(places):
            ref[s, b, pl.ds(r, 1)] = value[:, i * pair : (i + 1) * pair]

    def score_block(u, places, which):
        for n in range(heads):
            qv = rows_block(qx, u, n)
            top = jnp.full((8, lanes), FLOOR, F32)
            for i in range(chunks):
                rows = pl.ds((i % (chunks // 2)) * chunk, chunk)
                s = dot_nt(kb[i // (chunks // 2), rows, head(n)], qv) * (SCALE * LOG2E)
                s = s + bias[which, pl.ds(i * chunk, chunk)]
                sbuf[pl.ds(i * chunk, chunk)] = s
                top = jnp.maximum(top, jnp.max(s.reshape(chunk // 8, 8, lanes), axis=0))
            m = jnp.max(top, axis=0, keepdims=True)
            total = jnp.zeros((8, lanes), F32)
            for i in range(chunks):
                e = jnp.exp2(sbuf[pl.ds(i * chunk, chunk)] - m)
                total = total + jnp.sum(e.reshape(chunk // 8, 8, lanes), axis=0)
                probs[u, n, pl.ds(i * chunk, chunk)] = e.astype(BF16)
            total = jnp.maximum(jnp.sum(total, axis=0, keepdims=True), 1e-37)
            put(loc, places, n, m)
            put(loc, places, 4 + n, 1.0 / total)
            put(st, places, n, m + jnp.log2(total))

    k_load.wait()
    v_load.wait()
    for cp in q_copies:
        cp.wait()
    arrived(kb.at[1 - t], sib_s.at[0], sib_r.at[0])
    arrived(vb.at[1 - t], sib_s.at[1], sib_r.at[1])
    arrived(qx.at[4, :, 1 - t], sib_s.at[2], sib_r.at[2])
    arrived(qx.at[5, :, 1 - t], sib_s.at[3], sib_r.at[3])
    for n in range(heads):
        kt[n] = jnp.transpose(kb[:, :, head(n)].reshape(nk, HD))
    for g in range(2):
        score_block(4 + g, own(g), 1)

    w_load.wait()

    def d_send(i, c, d):
        return remote(
            down.at[i, :, part(c)],
            dx.at[i, 1 - d, t],
            d_s.at[i, d, c],
            d_r.at[i, 1 - d, t],
            (c, h - 1 + 2 * d, y),
        )

    def d_sib(i):
        return remote(
            down.at[i, :, other], dx.at[4 + i // 2, i % 2, t], d_s.at[i, 2, 0], d_r.at[i, 2, 0], sib
        )

    def d_own(i):
        return pltpu.make_async_copy(down.at[i, :, mine], dx.at[4 + i // 2, i % 2, t], lsem.at[9 + i])

    def project(i, count):
        src = gall[pl.ds(i, count)].reshape(count * shard, gall.shape[2])
        d = dot_nt(src, wall[...]).astype(BF16)
        down[pl.ds(i, count)] = d.reshape(count, shard, d.shape[1])

    def d_go(i):
        both(lambda d: [d_send(i, c, d).start() for c in range(2)])
        d_sib(i).start()
        d_own(i).start()

    def d_here(i):
        d_own(i).wait()
        arrived(dx.at[4 + i // 2, i % 2, 1 - t], d_s.at[i, 2, 0], d_r.at[i, 2, 0])

    def d_near(i):
        both(
            lambda d: [arrived(dx.at[i, d, tq], d_s.at[i, d, tq], d_r.at[i, d, tq]) for tq in range(2)]
        )

    project(0, 1)
    d_go(0)
    arrived(gall.at[2, first], g_s.at[0], g_r.at[0])
    arrived(gall.at[1, second], g_s.at[1], g_r.at[1])
    for cp in g_sends:
        cp.wait_send()
    for cp in g_relays:
        cp.start()
    arrived(gall.at[1, first], g_s.at[3], g_r.at[3])
    arrived(gall.at[2, second], g_s.at[2], g_r.at[2])
    project(1, 2)
    d_go(1)

    both(lambda d: [arrived(qx.at[pl.ds(0, 4), d, tq], q_s.at[d, tq], q_r.at[d, tq]) for tq in range(2)])

    @pl.loop(0, 4)
    def _(s):
        score_block(s, halo(s), 0)

    d_go(2)

    def exchange(own, got, ssem, rsem):
        def copies():
            return (
                (up, remote(own.at[pl.ds(0, 2)], got.at[pl.ds(3, 2)], ssem.at[0], rsem.at[1], (t, h - 1, y))),
                (dn, remote(own.at[pl.ds(1, 2)], got.at[pl.ds(1, 2)], ssem.at[1], rsem.at[0], (t, h + 1, y))),
                (up2, remote(own.at[0], got.at[5], ssem.at[2], rsem.at[3], (t, h - 2, y))),
                (dn2, remote(own.at[2], got.at[0], ssem.at[3], rsem.at[2], (t, h + 2, y))),
            )

        def go():
            for cond, cp in copies():
                pl.when(cond)(cp.start)

        def finish():
            for cond, cp in copies():
                pl.when(cond)(cp.wait_send)
            for cond, dst, i in (
                (up, got.at[pl.ds(1, 2)], 0),
                (dn, got.at[pl.ds(3, 2)], 1),
                (up2, got.at[0], 2),
                (dn2, got.at[5], 3),
            ):
                pl.when(cond)(lambda dst=dst, i=i: arrived(dst, ssem.at[i], rsem.at[i]))

        return go, finish

    swaps = [exchange(st.at[s], rv.at[s], st_s.at[s], st_r.at[s]) for s in range(4)]

    def delta_block(u, s, places, cols):
        size = cols.size
        for n in range(heads):
            if size == lanes:
                d = rows_block(dx, u, n)
            else:
                d = dx[u, s % 2, :, :, head(n)].reshape(pair, HD)
            total = jnp.zeros((8, size), F32)
            for i in range(chunks):
                rows = pl.ds((i % (chunks // 2)) * chunk, chunk)
                dp = dot_nt(vb[i // (chunks // 2), rows, head(n)], d)
                krows = pl.ds(i * chunk, chunk)
                dprobs[u, n, krows, cols] = dp
                x = dp * probs[u, n, krows, cols].astype(F32)
                total = total + jnp.sum(x.reshape(chunk // 8, 8, size), axis=0)
            total = jnp.sum(total, axis=0, keepdims=True)
            scale = [loc[k, b, pl.ds(4 + n, 1)] for k, b in places]
            scale = scale[0] if len(scale) == 1 else jnp.concatenate(scale, axis=1)
            put(st, places, 4 + n, total * scale)

    def deltas(s):
        d_here(s)
        delta_block(4 + s // 2, s, ((s, 1),), pl.ds((s % 2) * pair, pair))
        d_near(s)
        delta_block(s, s, halo(s), pl.ds(0, lanes))
        swaps[s][0]()

    def combine(s):
        swaps[s][1]()
        for b in range(3):
            x = [st[s, b], rv[s, 2 * b], rv[s, 2 * b + 1]]
            lse = [v[0:4] for v in x]
            top = jnp.maximum(jnp.maximum(lse[0], lse[1]), lse[2])
            weight = [jnp.exp2(v - top) for v in lse]
            total = weight[0] + weight[1] + weight[2]
            delta = (weight[0] * x[0][4:8] + weight[1] * x[1][4:8] + weight[2] * x[2][4:8]) / total
            c = jnp.exp2(loc[s, b, pl.ds(0, 4)] - (top + jnp.log2(total)))
            both_rows = jnp.concatenate([c, delta], axis=0)
            row[s, b] = both_rows
            col[s, b] = jnp.transpose(both_rows)

    def query_block(u, places):
        for n in range(heads):
            c, delta = [
                jnp.concatenate([row[s, b, pl.ds(r, 1)] for s, b in places], axis=1) for r in (n, 4 + n)
            ]
            ds = (probs[u, n].astype(F32) * (dprobs[u, n] - delta)).astype(BF16)
            dscores[u, n] = ds
            dqt = dot(kt[n], ds) * (c * SCALE)
            dq_part[u, :, :, :, head(n)] = jnp.transpose(dqt).astype(BF16).reshape(2, 2, shard, HD)

    def key_block(u, places):
        for n in range(heads):
            c = jnp.concatenate([col[s, b, :, pl.ds(n, 1)] for s, b in places], axis=0)
            dk_acc[n] += dot(dscores[u, n], (rows_block(qx, u, n).astype(F32) * c).astype(BF16))
            dv_acc[n] += dot(probs[u, n], (rows_block(dx, u, n).astype(F32) * c).astype(BF16))

    def p_send(s, j, tq):
        return remote(
            dq_part.at[s, j, tq],
            parts.at[t, 2 - 2 * j, s],
            p_s.at[s, j, tq],
            p_r.at[s, 1 - j, t],
            (tq, h - 1 + 2 * j, y),
        )

    def p_sib(g):
        return remote(
            dq_part.at[4 + g, :, 1 - t], parts.at[t, 1, pl.ds(2 * g, 2)], p_s.at[g, 2, 0], p_r.at[g, 2, 0], sib
        )

    def p_own(g):
        return pltpu.make_async_copy(dq_part.at[4 + g, :, t], parts.at[t, 1, pl.ds(2 * g, 2)], osem.at[4 + g])

    def give_back(s):
        combine(s)
        query_block(s, halo(s))
        both(lambda j: [p_send(s, j, tq).start() for tq in range(2)])

    def give_home(g):
        query_block(4 + g, own(g))
        p_sib(g).start()
        p_own(g).start()
        key_block(4 + g, own(g))

    deltas(0)
    arrived(gall.at[3, first], g_s.at[4], g_r.at[4])
    arrived(gall.at[3, second], g_s.at[5], g_r.at[5])
    project(3, 1)
    d_go(3)
    deltas(1)
    give_back(0)
    deltas(2)
    deltas(3)
    give_back(1)
    give_home(0)

    @pl.loop(0, 2)
    def _(s):
        key_block(s, halo(s))

    give_back(2)
    give_back(3)
    give_home(1)

    @pl.loop(2, 4)
    def _(s):
        key_block(s, halo(s))

    for n in range(heads):
        dv_low[:, :, head(n)] = dv_acc[n].astype(BF16).reshape(2, tile, HD)
        dk_low[:, :, head(n)] = (dk_acc[n] * SCALE).astype(BF16).reshape(2, tile, HD)
    dv_sib = remote(dv_low.at[1 - t], dv_hbm.at[:, mine], e_s.at[0], e_r.at[0], sib)
    dk_sib = remote(dk_low.at[1 - t], dk_hbm.at[:, mine], e_s.at[1], e_r.at[1], sib)
    dv_sib.start()
    dk_sib.start()
    dv_out = pltpu.make_async_copy(dv_low.at[t], dv_hbm.at[:, mine], osem.at[0])
    dk_out = pltpu.make_async_copy(dk_low.at[t], dk_hbm.at[:, mine], osem.at[1])
    dv_out.start()
    dk_out.start()

    for g in range(2):
        p_own(g).wait()
        arrived(parts.at[1 - t, 1, pl.ds(2 * g, 2)], p_s.at[g, 2, 0], p_r.at[g, 2, 0])
    for s in range(4):
        both(
            lambda d, s=s: [arrived(parts.at[c, 2 * d, s], p_s.at[s, d, c], p_r.at[s, d, c]) for c in range(2)]
        )

    @pl.when(h == 0)
    def _():
        for c in range(2):
            zero_part(0, c).wait()

    @pl.when(h == heights - 1)
    def _():
        for c in range(2):
            zero_part(2, c).wait()

    for cp in g_relays + sib_sends:
        cp.wait_send()
    both(lambda d: [q_send(c, d).wait_send() for c in range(2)])
    for i in range(4):
        both(lambda d, i=i: [d_send(i, c, d).wait_send() for c in range(2)])
        d_sib(i).wait_send()
    for s in range(4):
        both(lambda d, s=s: [p_send(s, d, tq).wait_send() for tq in range(2)])
    for g in range(2):
        p_sib(g).wait_send()
    dv_sib.wait_send()
    dk_sib.wait_send()
    arrived(dv_hbm.at[:, other], e_s.at[0], e_r.at[0])
    arrived(dk_hbm.at[:, other], e_s.at[1], e_r.at[1])
    dv_out.wait()
    dk_out.wait()


def finish(parts, dk, dv, dq_hbm, dk_hbm, dv_hbm, buf, dk_buf, dv_buf, dq_out, sem):
    y = lax.axis_index("tensor")
    shard, half = buf.shape[4:]
    loads = [
        pltpu.make_async_copy(parts.at[:, :, pl.ds(0, 2)], buf.at[0], sem.at[0]),
        pltpu.make_async_copy(parts.at[:, :, pl.ds(2, 2)], buf.at[1], sem.at[1]),
        pltpu.make_async_copy(dk, dk_buf, sem.at[2]),
        pltpu.make_async_copy(dv, dv_buf, sem.at[3]),
    ]
    stores = [
        pltpu.make_async_copy(dk_buf, dk_hbm, sem.at[4]),
        pltpu.make_async_copy(dv_buf, dv_hbm, sem.at[5]),
    ]
    for k in range(4):
        rows = pl.ds(pl.multiple_of(lax.rem(y + SHARD[k], 4) * shard, shard), shard)
        stores.append(
            pltpu.make_async_copy(
                dq_out.at[k], dq_hbm.at[rows], sem.at[6 + k]
            )
        )
    for i in (2, 3, 0, 1):
        loads[i].start()
    for i in range(2):
        loads[2 + i].wait()
        stores[i].start()
    for g in range(2):
        loads[g].wait()
        for c in range(2):
            x = buf[g, c, 0].astype(F32) + buf[g, c, 1].astype(F32) + buf[g, c, 2].astype(F32)
            dq_out[pl.ds(2 * g, 2), :, pl.ds(c * half, half)] = x.astype(BF16)
        stores[2 + 2 * g].start()
        stores[3 + 2 * g].start()
    for cp in stores:
        cp.wait()


def local(queries, key_rows, value_rows, grad_output, out_weight, window_flags, valid_counts):
    tile, width = queries.shape[3:]
    model = grad_output.shape[-1]
    half = width // 2
    heads = half // HD
    shard = tile // 4
    pair, lanes, nk = 2 * shard, 4 * shard, 2 * tile
    heights = lax.axis_size("height")
    shape = jax.ShapeDtypeStruct((tile, width), BF16)
    parts_shape = jax.ShapeDtypeStruct((2, 3, 4, shard, half), BF16)
    any_spec = pl.BlockSpec(memory_space=pl.ANY)
    dma = pltpu.SemaphoreType.DMA
    vm = pltpu.VMEM
    outs = pl.pallas_call(
        lambda *refs: kernel(heights, *refs),
        out_shape=(parts_shape, shape, shape),
        in_specs=[any_spec] * 7,
        out_specs=(any_spec, any_spec, any_spec),
        scratch_shapes=[
            vm((2, 9, 1, heights), jnp.int32),
            vm((2, 1, heights), jnp.int32),
            vm((4, shard, width), BF16),
            vm((4, shard, width), BF16),
            vm((4, shard, model), BF16),
            vm((width, model), BF16),
            vm((6, 2, 2, shard, half), BF16),
            vm((6, 2, 2, shard, half), BF16),
            vm((2, tile, half), BF16),
            vm((2, tile, half), BF16),
            vm((heads, HD, nk), BF16),
            vm((2, nk, lanes), F32),
            vm((nk, lanes), F32),
            vm((6, heads, nk, lanes), BF16),
            vm((6, heads, nk, lanes), F32),
            vm((6, heads, nk, lanes), BF16),
            vm((heads, nk, HD), F32),
            vm((heads, nk, HD), F32),
            vm((2, tile, half), BF16),
            vm((2, tile, half), BF16),
            vm((6, 2, 2, shard, half), BF16),
            vm((4, 3, 8, pair), F32),
            vm((4, 6, 8, pair), F32),
            vm((4, 3, 8, pair), F32),
            vm((4, 3, 8, pair), F32),
            vm((4, 3, pair, 8), F32),
            dma((16,)),
            dma((6,)),
            dma((6,)),
            dma((6,)),
            dma((2, 2)),
            dma((2, 2)),
            dma((4,)),
            dma((4,)),
            dma((4, 3, 2)),
            dma((4, 3, 2)),
            dma((4, 4)),
            dma((4, 4)),
            dma((4, 3, 2)),
            dma((4, 3, 2)),
            dma((2,)),
            dma((2,)),
        ],
        compiler_params=pltpu.CompilerParams(
            collective_id=0, has_side_effects=True, vmem_limit_bytes=56 * 2**20
        ),
    )(
        window_flags.transpose(0, 3, 2, 1),
        valid_counts.transpose(0, 2, 1),
        queries.reshape(tile, width),
        key_rows.reshape(tile, width),
        value_rows.reshape(tile, width),
        grad_output.reshape(grad_output.shape[3], model),
        out_weight,
    )
    outs = pl.pallas_call(
        finish,
        out_shape=(shape, shape, shape),
        in_specs=[any_spec] * 3,
        out_specs=(any_spec,) * 3,
        scratch_shapes=[
            vm((2, 2, 3, 2, shard, half), BF16),
            vm((tile, width), BF16),
            vm((tile, width), BF16),
            vm((4, shard, width), BF16),
            dma((10,)),
        ],
    )(*outs)
    return tuple(x.reshape(queries.shape) for x in outs)


def solution(mesh):
    wide = P("tm", "height", None, None, "tensor")
    placed = (wide, wide, wide, P("tm", "height", None, "tensor", None), P("tensor", None), P(), P())
    return jax.shard_map(local, mesh=mesh, in_specs=placed, out_specs=(wide, wide, wide), check_vma=False)
```

time: 48.6 us -> 46.5 us (0.957)
  the two profiles are of different devices: /device:TPU:129 before, /device:TPU:103 now
where the time goes in v4:
time: 46.5 us; the launch traced here: 46.3 us
  Pallas kernels  45.7 us (98%)
  between operations  0.64 us (1%)
    pallas_call x1, Pallas kernels, local(): pl.pallas_call(lambda *refs: kernel(heights, *refs), out_shape=(parts_sha...  43.4 us
    pallas_call x1, Pallas kernels, local(): pl.pallas_call(finish, out_shape=(shape, shape, shape), in_specs=[any_spe...  2.32 us

profile of v4, /device:TPU:103, one launch (start us, length us, event | category | flops | bytes accessed | tf_op | source)
XLA Modules:
  0.0 46.3 jit_solution(1170380700522518035)
XLA Ops:
  0.6 43.4 %shard_map.94 = (bf16[2,3,4,64,384]{4,3,2,1,0:T(8,128)(2,1)}, bf16[256,768]{1,0:T(8,128)(2,1)}, bf16[256,768]{1,0:T(8,128)(2,1)}) custom-call(s32[2,9,1,32]{3,2,1,0:T(1,128)} %bitcast.15, s32[2,1,32]{2,1,0:T(1,128)} %bitcast.16, bf16[256,768]{1,0:T(8,128)(2,1)} %bitcast.11, bf16[256,768]{1,0:T(8,128)(2,1)} %bitcast.12, bf16[256,768]{1,0:T(8,128)(2,1)} %bitcast.13, ...), custom_call_target="tpu_custom_call" | custom-call | tf_op jit(solution)/shard_map/pallas_call | solution.py:637
  44.0 2.3 %shard_map.95 = (bf16[256,768]{1,0:T(8,128)(2,1)}, bf16[256,768]{1,0:T(8,128)(2,1)}, bf16[256,768]{1,0:T(8,128)(2,1)}) custom-call(bf16[2,3,4,64,384]{4,3,2,1,0:T(8,128)(2,1)} %get-tuple-element.9.parts, bf16[256,768]{1,0:T(8,128)(2,1)} %get-tuple-element.10.dk, bf16[256,768]{1,0:T(8,128)(2,1)} %get-tuple-element.11.dv), custom_call_target="tpu_custom_call" | custom-call | tf_op jit(solution)/shard_map/pallas_call | solution.py:698

commit v5 on v4

--- a/solution.py
+++ b/solution.py
@@ -43,6 +43,7 @@
     down,
     gall,
     wall,
+    wt,
     qx,
     dx,
     kb,
@@ -287,7 +288,7 @@
     for cp in q_copies:
         cp.start()
 
-    chunk = 128
+    chunk = 256
     nk = 2 * tile
     chunks = nk // chunk
 
@@ -342,6 +343,8 @@
         score_block(4 + g, own(g), 1)
 
     w_load.wait()
+    for i in range(0, wt.shape[0], 512):
+        wt[pl.ds(i, 512)] = jnp.transpose(wall[:, pl.ds(i, 512)])
 
     def d_send(i, c, d):
         return remote(
@@ -362,7 +365,7 @@
 
     def project(i, count):
         src = gall[pl.ds(i, count)].reshape(count * shard, gall.shape[2])
-        d = dot_nt(src, wall[...]).astype(BF16)
+        d = dot(src, wt[...]).astype(BF16)
         down[pl.ds(i, count)] = d.reshape(count, shard, d.shape[1])
 
     def d_go(i):
@@ -511,7 +514,6 @@
         query_block(4 + g, own(g))
         p_sib(g).start()
         p_own(g).start()
-        key_block(4 + g, own(g))
 
     deltas(0)
     arrived(gall.at[3, first], g_s.at[4], g_r.at[4])
@@ -521,21 +523,18 @@
     deltas(1)
     give_back(0)
     deltas(2)
+    key_block(0, halo(0))
     deltas(3)
     give_back(1)
+    key_block(1, halo(1))
     give_home(0)
-
-    @pl.loop(0, 2)
-    def _(s):
-        key_block(s, halo(s))
-
+    key_block(4, own(0))
     give_back(2)
+    key_block(2, halo(2))
     give_back(3)
     give_home(1)
-
-    @pl.loop(2, 4)
-    def _(s):
-        key_block(s, halo(s))
+    key_block(5, own(1))
+    key_block(3, halo(3))
 
     for n in range(heads):
         dv_low[:, :, head(n)] = dv_acc[n].astype(BF16).reshape(2, tile, HD)
@@ -646,6 +645,7 @@
             vm((4, shard, width), BF16),
             vm((4, shard, model), BF16),
             vm((width, model), BF16),
+            vm((model, width), BF16),
             vm((6, 2, 2, shard, half), BF16),
             vm((6, 2, 2, shard, half), BF16),
             vm((2, tile, half), BF16),

time: 46.5 us -> 44.8 us (0.963)
  the two profiles are of different devices: /device:TPU:103 before, /device:TPU:129 now
where the time goes in v5:
time: 44.8 us; the launch traced here: 44.6 us
  Pallas kernels  43.8 us (98%)
  between operations  0.8 us (2%)
    pallas_call x1, Pallas kernels, local(): pl.pallas_call(lambda *refs: kernel(heights, *refs), out_shape=(parts_sha...  41.5 us
    pallas_call x1, Pallas kernels, local(): pl.pallas_call(finish, out_shape=(shape, shape, shape), in_specs=[any_spe...  2.32 us

profile of v5, /device:TPU:129, one launch (start us, length us, event | category | flops | bytes accessed | tf_op | source)
XLA Modules:
  0.0 44.6 jit_solution(16906552176067942221)
XLA Ops:
  0.6 41.5 %shard_map.94 = (bf16[2,3,4,64,384]{4,3,2,1,0:T(8,128)(2,1)}, bf16[256,768]{1,0:T(8,128)(2,1)}, bf16[256,768]{1,0:T(8,128)(2,1)}) custom-call(s32[2,9,1,32]{3,2,1,0:T(1,128)} %bitcast.15, s32[2,1,32]{2,1,0:T(1,128)} %bitcast.16, bf16[256,768]{1,0:T(8,128)(2,1)} %bitcast.11, bf16[256,768]{1,0:T(8,128)(2,1)} %bitcast.12, bf16[256,768]{1,0:T(8,128)(2,1)} %bitcast.13, ...), custom_call_target="tpu_custom_call" | custom-call | tf_op jit(solution)/shard_map/pallas_call | solution.py:636
  42.1 2.3 %shard_map.95 = (bf16[256,768]{1,0:T(8,128)(2,1)}, bf16[256,768]{1,0:T(8,128)(2,1)}, bf16[256,768]{1,0:T(8,128)(2,1)}) custom-call(bf16[2,3,4,64,384]{4,3,2,1,0:T(8,128)(2,1)} %get-tuple-element.9.parts, bf16[256,768]{1,0:T(8,128)(2,1)} %get-tuple-element.10.dk, bf16[256,768]{1,0:T(8,128)(2,1)} %get-tuple-element.11.dv), custom_call_target="tpu_custom_call" | custom-call | tf_op jit(solution)/shard_map/pallas_call | solution.py:698

commit v6 on v5

--- a/solution.py
+++ b/solution.py
@@ -152,6 +152,69 @@
     def _():
         greet((t, h + 2, y))
 
+    pl.semaphore_wait(
+        barrier,
+        4
+        + 2 * up.astype(jnp.int32)
+        + 2 * dn.astype(jnp.int32)
+        + up2.astype(jnp.int32)
+        + dn2.astype(jnp.int32),
+    )
+
+    ahead, behind = (t, h, lax.rem(y + 1, 4)), (t, h, lax.rem(y + 3, 4))
+    first, second = pl.ds(0, shard // 2), pl.ds(shard // 2, shard // 2)
+    g_sends = [
+        remote(g_hbm.at[first], gall.at[2, first], g_s.at[0], g_r.at[0], ahead),
+        remote(g_hbm.at[second], gall.at[1, second], g_s.at[1], g_r.at[1], behind),
+        remote(g_hbm.at[second], gall.at[2, second], g_s.at[2], g_r.at[2], ahead),
+        remote(g_hbm.at[first], gall.at[1, first], g_s.at[3], g_r.at[3], behind),
+    ]
+    g_relays = [
+        remote(gall.at[2, first], gall.at[3, first], g_s.at[4], g_r.at[4], ahead),
+        remote(gall.at[1, second], gall.at[3, second], g_s.at[5], g_r.at[5], behind),
+    ]
+    for cp in g_sends:
+        cp.start()
+    for cp in q_loads:
+        cp.wait()
+    def part(c):
+        return pl.ds(c * half, half)
+
+    def q_send(c, d):
+        return remote(
+            qown.at[:, :, part(c)],
+            qx.at[pl.ds(0, 4), 1 - d, t],
+            q_s.at[d, c],
+            q_r.at[1 - d, t],
+            (c, h - 1 + 2 * d, y),
+        )
+
+    def both(fn):
+        @pl.when(up)
+        def _():
+            fn(0)
+
+        @pl.when(dn)
+        def _():
+            fn(1)
+
+    both(lambda d: [q_send(c, d).start() for c in range(2)])
+    sib_sends = [
+        remote(k_hbm.at[:, other], kb.at[t], sib_s.at[0], sib_r.at[0], sib),
+        remote(v_hbm.at[:, other], vb.at[t], sib_s.at[1], sib_r.at[1], sib),
+        remote(qown.at[pl.ds(0, 2), :, other], qx.at[4, :, t], sib_s.at[2], sib_r.at[2], sib),
+        remote(qown.at[pl.ds(2, 2), :, other], qx.at[5, :, t], sib_s.at[3], sib_r.at[3], sib),
+    ]
+    for cp in sib_sends:
+        cp.start()
+
+    q_copies = [
+        pltpu.make_async_copy(qown.at[pl.ds(2 * g, 2), :, mine], qx.at[4 + g, :, t], lsem.at[(8, 15)[g]])
+        for g in range(2)
+    ]
+    for cp in q_copies:
+        cp.start()
+
     def zero_part(b, c):
         return pltpu.make_async_copy(dx.at[pl.ds(0, 4), b // 2, c], parts.at[c, b], osem.at[2 + c])
 
@@ -223,70 +286,6 @@
                 bias[1, krows, pl.ds(pair, pair)] = value
             else:
                 bias[0, krows, pl.ds((b // 2) * pair, pair)] = value
-
-    pl.semaphore_wait(
-        barrier,
-        4
-        + 2 * up.astype(jnp.int32)
-        + 2 * dn.astype(jnp.int32)
-        + up2.astype(jnp.int32)
-        + dn2.astype(jnp.int32),
-    )
-
-    g_load.wait()
-    ahead, behind = (t, h, lax.rem(y + 1, 4)), (t, h, lax.rem(y + 3, 4))
-    first, second = pl.ds(0, shard // 2), pl.ds(shard // 2, shard // 2)
-    g_sends = [
-        remote(gall.at[0, first], gall.at[2, first], g_s.at[0], g_r.at[0], ahead),
-        remote(gall.at[0, second], gall.at[1, second], g_s.at[1], g_r.at[1], behind),
-        remote(gall.at[0, second], gall.at[2, second], g_s.at[2], g_r.at[2], ahead),
-        remote(gall.at[0, first], gall.at[1, first], g_s.at[3], g_r.at[3], behind),
-    ]
-    g_relays = [
-        remote(gall.at[2, first], gall.at[3, first], g_s.at[4], g_r.at[4], ahead),
-        remote(gall.at[1, second], gall.at[3, second], g_s.at[5], g_r.at[5], behind),
-    ]
-    for cp in g_sends:
-        cp.start()
-    for cp in q_loads:
-        cp.wait()
-    sib_sends = [
-        remote(k_hbm.at[:, other], kb.at[t], sib_s.at[0], sib_r.at[0], sib),
-        remote(v_hbm.at[:, other], vb.at[t], sib_s.at[1], sib_r.at[1], sib),
-        remote(qown.at[pl.ds(0, 2), :, other], qx.at[4, :, t], sib_s.at[2], sib_r.at[2], sib),
-        remote(qown.at[pl.ds(2, 2), :, other], qx.at[5, :, t], sib_s.at[3], sib_r.at[3], sib),
-    ]
-    for cp in sib_sends:
-        cp.start()
-
-    def part(c):
-        return pl.ds(c * half, half)
-
-    def q_send(c, d):
-        return remote(
-            qown.at[:, :, part(c)],
-            qx.at[pl.ds(0, 4), 1 - d, t],
-            q_s.at[d, c],
-            q_r.at[1 - d, t],
-            (c, h - 1 + 2 * d, y),
-        )
-
-    def both(fn):
-        @pl.when(up)
-        def _():
-            fn(0)
-
-        @pl.when(dn)
-        def _():
-            fn(1)
-
-    both(lambda d: [q_send(c, d).start() for c in range(2)])
-    q_copies = [
-        pltpu.make_async_copy(qown.at[pl.ds(2 * g, 2), :, mine], qx.at[4 + g, :, t], lsem.at[(8, 15)[g]])
-        for g in range(2)
-    ]
-    for cp in q_copies:
-        cp.start()
 
     chunk = 256
     nk = 2 * tile
@@ -373,6 +372,13 @@
         d_sib(i).start()
         d_own(i).start()
 
+    def project_far():
+        for c in range(2):
+            down[3, :, part(c)] = dot(gall[3], wt[:, part(c)]).astype(BF16)
+            both(lambda d, c=c: d_send(3, c, d).start())
+        d_sib(3).start()
+        d_own(3).start()
+
     def d_here(i):
         d_own(i).wait()
         arrived(dx.at[4 + i // 2, i % 2, 1 - t], d_s.at[i, 2, 0], d_r.at[i, 2, 0])
@@ -382,6 +388,7 @@
             lambda d: [arrived(dx.at[i, d, tq], d_s.at[i, d, tq], d_r.at[i, d, tq]) for tq in range(2)]
         )
 
+    g_load.wait()
     project(0, 1)
     d_go(0)
     arrived(gall.at[2, first], g_s.at[0], g_r.at[0])
@@ -394,6 +401,7 @@
     arrived(gall.at[2, second], g_s.at[2], g_r.at[2])
     project(1, 2)
     d_go(1)
+    d_go(2)
 
     both(lambda d: [arrived(qx.at[pl.ds(0, 4), d, tq], q_s.at[d, tq], q_r.at[d, tq]) for tq in range(2)])
 
@@ -401,7 +409,6 @@
     def _(s):
         score_block(s, halo(s), 0)
 
-    d_go(2)
 
     def exchange(own, got, ssem, rsem):
         def copies():
@@ -468,9 +475,7 @@
             total = weight[0] + weight[1] + weight[2]
             delta = (weight[0] * x[0][4:8] + weight[1] * x[1][4:8] + weight[2] * x[2][4:8]) / total
             c = jnp.exp2(loc[s, b, pl.ds(0, 4)] - (top + jnp.log2(total)))
-            both_rows = jnp.concatenate([c, delta], axis=0)
-            row[s, b] = both_rows
-            col[s, b] = jnp.transpose(both_rows)
+            row[s, b] = jnp.concatenate([c, delta], axis=0)
 
     def query_block(u, places):
         for n in range(heads):
@@ -509,6 +514,8 @@
         combine(s)
         query_block(s, halo(s))
         both(lambda j: [p_send(s, j, tq).start() for tq in range(2)])
+        for b in range(3):
+            col[s, b] = jnp.transpose(row[s, b])
 
     def give_home(g):
         query_block(4 + g, own(g))
@@ -518,8 +525,7 @@
     deltas(0)
     arrived(gall.at[3, first], g_s.at[4], g_r.at[4])
     arrived(gall.at[3, second], g_s.at[5], g_r.at[5])
-    project(3, 1)
-    d_go(3)
+    project_far()
     deltas(1)
     give_back(0)
     deltas(2)

time: 44.8 us -> 43.6 us (0.973)
  Pallas kernels: 43.8 us -> 42.6 us
    pallas_call x1, Pallas kernels: 41.5 us -> 40.3 us  [local(): pl.pallas_call(lambda *refs: kernel(heights, *refs), out_shape=(parts_sha...]
where the time goes in v6:
time: 43.6 us; the launch traced here: 43.5 us
  Pallas kernels  42.6 us (98%)
  between operations  0.8 us (2%)
    pallas_call x1, Pallas kernels, local(): pl.pallas_call(lambda *refs: kernel(heights, *refs), out_shape=(parts_sha...  40.3 us
    pallas_call x1, Pallas kernels, local(): pl.pallas_call(finish, out_shape=(shape, shape, shape), in_specs=[any_spe...  2.32 us

profile of v6, /device:TPU:129, one launch (start us, length us, event | category | flops | bytes accessed | tf_op | source)
XLA Modules:
  0.0 43.5 jit_solution(14507799614703873685)
XLA Ops:
  0.6 40.3 %shard_map.94 = (bf16[2,3,4,64,384]{4,3,2,1,0:T(8,128)(2,1)}, bf16[256,768]{1,0:T(8,128)(2,1)}, bf16[256,768]{1,0:T(8,128)(2,1)}) custom-call(s32[2,9,1,32]{3,2,1,0:T(1,128)} %bitcast.15, s32[2,1,32]{2,1,0:T(1,128)} %bitcast.16, bf16[256,768]{1,0:T(8,128)(2,1)} %bitcast.11, bf16[256,768]{1,0:T(8,128)(2,1)} %bitcast.12, bf16[256,768]{1,0:T(8,128)(2,1)} %bitcast.13, ...), custom_call_target="tpu_custom_call" | custom-call | tf_op jit(solution)/shard_map/pallas_call | solution.py:642
  41.0 2.3 %shard_map.95 = (bf16[256,768]{1,0:T(8,128)(2,1)}, bf16[256,768]{1,0:T(8,128)(2,1)}, bf16[256,768]{1,0:T(8,128)(2,1)}) custom-call(bf16[2,3,4,64,384]{4,3,2,1,0:T(8,128)(2,1)} %get-tuple-element.9.parts, bf16[256,768]{1,0:T(8,128)(2,1)} %get-tuple-element.10.dk, bf16[256,768]{1,0:T(8,128)(2,1)} %get-tuple-element.11.dv), custom_call_target="tpu_custom_call" | custom-call | tf_op jit(solution)/shard_map/pallas_call | solution.py:704

commit v7 on v6

--- a/solution.py
+++ b/solution.py
@@ -180,12 +180,12 @@
     def part(c):
         return pl.ds(c * half, half)
 
-    def q_send(c, d):
+    def q_send(p, c, d):
         return remote(
-            qown.at[:, :, part(c)],
-            qx.at[pl.ds(0, 4), 1 - d, t],
-            q_s.at[d, c],
-            q_r.at[1 - d, t],
+            qown.at[pl.ds(2 * p, 2), :, part(c)],
+            qx.at[pl.ds(2 * p, 2), 1 - d, t],
+            q_s.at[p, d, c],
+            q_r.at[p, 1 - d, t],
             (c, h - 1 + 2 * d, y),
         )
 
@@ -198,7 +198,7 @@
         def _():
             fn(1)
 
-    both(lambda d: [q_send(c, d).start() for c in range(2)])
+    both(lambda d: [q_send(0, c, d).start() for c in range(2)])
     sib_sends = [
         remote(k_hbm.at[:, other], kb.at[t], sib_s.at[0], sib_r.at[0], sib),
         remote(v_hbm.at[:, other], vb.at[t], sib_s.at[1], sib_r.at[1], sib),
@@ -391,6 +391,20 @@
     g_load.wait()
     project(0, 1)
     d_go(0)
+    both(lambda d: [q_send(1, c, d).start() for c in range(2)])
+
+    def halo_scores(p):
+        both(
+            lambda d: [
+                arrived(qx.at[pl.ds(2 * p, 2), d, tq], q_s.at[p, d, tq], q_r.at[p, d, tq]) for tq in range(2)
+            ]
+        )
+
+        @pl.loop(2 * p, 2 * p + 2)
+        def _(s):
+            score_block(s, halo(s), 0)
+
+    halo_scores(0)
     arrived(gall.at[2, first], g_s.at[0], g_r.at[0])
     arrived(gall.at[1, second], g_s.at[1], g_r.at[1])
     for cp in g_sends:
@@ -402,13 +416,6 @@
     project(1, 2)
     d_go(1)
     d_go(2)
-
-    both(lambda d: [arrived(qx.at[pl.ds(0, 4), d, tq], q_s.at[d, tq], q_r.at[d, tq]) for tq in range(2)])
-
-    @pl.loop(0, 4)
-    def _(s):
-        score_block(s, halo(s), 0)
-
 
     def exchange(own, got, ssem, rsem):
         def copies():
@@ -523,6 +530,7 @@
         p_own(g).start()
 
     deltas(0)
+    halo_scores(1)
     arrived(gall.at[3, first], g_s.at[4], g_r.at[4])
     arrived(gall.at[3, second], g_s.at[5], g_r.at[5])
     project_far()
@@ -574,7 +582,8 @@
 
     for cp in g_relays + sib_sends:
         cp.wait_send()
-    both(lambda d: [q_send(c, d).wait_send() for c in range(2)])
+    for p in range(2):
+        both(lambda d, p=p: [q_send(p, c, d).wait_send() for c in range(2)])
     for i in range(4):
         both(lambda d, i=i: [d_send(i, c, d).wait_send() for c in range(2)])
         d_sib(i).wait_send()
@@ -676,8 +685,8 @@
             dma((6,)),
             dma((6,)),
             dma((6,)),
-            dma((2, 2)),
-            dma((2, 2)),
+            dma((2, 2, 2)),
+            dma((2, 2, 2)),
             dma((4,)),
             dma((4,)),
             dma((4, 3, 2)),

time: 43.6 us -> 42.8 us (0.982)
  Pallas kernels: 42.6 us -> 41.7 us
    pallas_call x1, Pallas kernels: 40.3 us -> 39.3 us  [local(): pl.pallas_call(lambda *refs: kernel(heights, *refs), out_shape=(parts_sha...]
where the time goes in v7:
time: 42.8 us; the launch traced here: 42.5 us
  Pallas kernels  41.7 us (97%)
  between operations  0.8 us (2%)
    pallas_call x1, Pallas kernels, local(): pl.pallas_call(lambda *refs: kernel(heights, *refs), out_shape=(parts_sha...  39.3 us
    pallas_call x1, Pallas kernels, local(): pl.pallas_call(finish, out_shape=(shape, shape, shape), in_specs=[any_spe...  2.32 us

profile of v7, /device:TPU:129, one launch (start us, length us, event | category | flops | bytes accessed | tf_op | source)
XLA Modules:
  0.0 42.5 jit_solution(6984864878430336863)
XLA Ops:
  0.6 39.3 %shard_map.94 = (bf16[2,3,4,64,384]{4,3,2,1,0:T(8,128)(2,1)}, bf16[256,768]{1,0:T(8,128)(2,1)}, bf16[256,768]{1,0:T(8,128)(2,1)}) custom-call(s32[2,9,1,32]{3,2,1,0:T(1,128)} %bitcast.15, s32[2,1,32]{2,1,0:T(1,128)} %bitcast.16, bf16[256,768]{1,0:T(8,128)(2,1)} %bitcast.11, bf16[256,768]{1,0:T(8,128)(2,1)} %bitcast.12, bf16[256,768]{1,0:T(8,128)(2,1)} %bitcast.13, ...), custom_call_target="tpu_custom_call" | custom-call | tf_op jit(solution)/shard_map/pallas_call | solution.py:651
  40.0 2.3 %shard_map.95 = (bf16[256,768]{1,0:T(8,128)(2,1)}, bf16[256,768]{1,0:T(8,128)(2,1)}, bf16[256,768]{1,0:T(8,128)(2,1)}) custom-call(bf16[2,3,4,64,384]{4,3,2,1,0:T(8,128)(2,1)} %get-tuple-element.9.parts, bf16[256,768]{1,0:T(8,128)(2,1)} %get-tuple-element.10.dk, bf16[256,768]{1,0:T(8,128)(2,1)} %get-tuple-element.11.dv), custom_call_target="tpu_custom_call" | custom-call | tf_op jit(solution)/shard_map/pallas_call | solution.py:713
